TPU v7x, 512 devices: a whole 4x4x16 slice. The times are simulated.
512 devices in a mesh: rows: 64 (over z, y), cols: 8 (over x, core).
Axes of the slice: x: 4, y: 4, z: 16, core: 2. Of those that a mesh axis runs over, the one named last changes fastest.
Arguments:
- snapshots: bfloat16 [131072, 2048], P('rows', 'cols')
- orient: int32 [3, 8], P(None, 'cols'), may hold values 0 or 1
Outputs:
- rotated: bfloat16 [131072, 2048], P('rows', 'cols')
- column_rms: float32 [2048], P('cols')
All inputs are finite; a program needn't handle non-finite values. No bound on the sum of `orient` on one device may be relied on, other than what follows from the above.
Results may differ from a plain program's by a relative error of at most 0.011.
Values may be sent and summed in bfloat16 or wider, within the bound.
No kernel may reach another device: no remote copies, remote signals or barrier semaphores. Data moves between devices by JAX's collectives and lax.ppermute only.
A program may use at most 64 MiB of HBM per device.

v0:
```python
import jax
import jax.numpy as jnp
from jax import lax
from jax.sharding import PartitionSpec as P

ROUNDS = 3
POLAR_ITERS = 12


def passed_along(value, axis, steps):
    count = lax.axis_size(axis)
    first, last = (max(0, -steps), min(count, count - steps))
    return lax.ppermute(value, axis, [(source, source + steps) for source in range(first, last)])


def inner(left, right):
    return lax.dot_general(
        left, right, (((0,), (0,)), ((), ())), preferred_element_type=jnp.float32
    )


def polar(gram):
    order = gram.shape[0]
    trace_mean = jnp.trace(gram) / order + 1e-06
    upper_part = jnp.triu(gram / trace_mean, 1)
    generator = upper_part - upper_part.T
    initial = jnp.eye(order, dtype=jnp.float32) + 0.5 * generator
    initial = initial / jnp.sqrt(jnp.sum(initial * initial))

    def refine(sweep, iterate):
        square = jnp.dot(iterate.T, iterate, precision=lax.Precision.HIGHEST)
        return 1.5 * iterate - 0.5 * jnp.dot(iterate, square, precision=lax.Precision.HIGHEST)

    return lax.fori_loop(0, POLAR_ITERS, refine, initial).astype(jnp.bfloat16)


def per_device(snapshots, orient):
    block_width = snapshots.shape[1] // 2
    upper_block = snapshots[:, :block_width]
    lower_block = snapshots[:, block_width:]
    position = lax.axis_index("cols")
    cycle_size = lax.axis_size("cols")
    for round_index in range(ROUNDS):
        flipped = orient[round_index, 0] == 1
        first = jnp.where(flipped, lower_block, upper_block)
        second = jnp.where(flipped, upper_block, lower_block)
        paired = jnp.concatenate([first, second], axis=1)
        gram = lax.psum(inner(paired, paired), "rows")
        turned = jnp.dot(paired, polar(gram), preferred_element_type=jnp.float32).astype(
            jnp.bfloat16
        )
        first = turned[:, :block_width]
        second = turned[:, block_width:]
        upper_block = jnp.where(flipped, second, first)
        lower_block = jnp.where(flipped, first, second)
        if round_index + 1 < ROUNDS:
            upward = jnp.where(position == 0, lower_block, upper_block)
            climbed = passed_along(upward, "cols", 1)
            descended = passed_along(lower_block, "cols", -1)
            new_upper = jnp.where(position == 0, upper_block, climbed)
            new_lower = jnp.where(position == cycle_size - 1, upper_block, descended)
            upper_block, lower_block = (new_upper, new_lower)
    rotated = jnp.concatenate([upper_block, lower_block], axis=1)
    wide = rotated.astype(jnp.float32)
    squares_sum = lax.psum(jnp.sum(wide * wide, axis=0), "rows")
    column_rms = jnp.sqrt(squares_sum / (snapshots.shape[0] * lax.axis_size("rows")))
    return (rotated, column_rms)


def solution(mesh):
    in_specs = (P("rows", "cols"), P(None, "cols"))
    out_specs = (P("rows", "cols"), P("cols"))
    return jax.shard_map(
        per_device, mesh=mesh, in_specs=in_specs, out_specs=out_specs, check_vma=False
    )
```

profile of v0, /device:TPU:4, one launch (start us, length us, event | category | flops | bytes accessed | tf_op | source)
XLA Modules:
  0.0 1024.5 jit_solution(100899449648917830)
XLA Ops:
  7.2 1.4 fusion.22
  8.6 1.3 fusion.21
  11.0 1.2 fusion.8
  12.7 266.8 %all-reduce.4.cloned.1.call-done = f32[256,256]{1,0:T(8,128)} async-done(((f32[256,256]{1,0:T(8,128)}), f32[256,256]{1,0:T(8,128)}) %all-reduce.4.cloned.1.call-update) | async-done | bytes 262160 | tf_op jit(solution)/shard_map/psum | solution.py:48
  279.5 1.1 copy.7
  280.5 0.6 select_reduce_fusion.2
  281.8 1.0 divide_select_fusion.2
  283.0 0.7 multiply_reduce_fusion.3
  284.5 12.8 %while.30 = (s32[]{:T(128)}, f32[256,256]{0,1:T(8,128)S(1)}, s32[]{:T(128)}) while((s32[]{:T(128)}, f32[256,256]{0,1:T(8,128)S(1)}, s32[]{:T(128)}) %tuple.63), condition=%wide.region_4.5_spmd, body=%wide.region_3.4_spmd.sunk | while | flops 402849792 | bytes 1835053 | solution.py:34
  285.0 0.6 fusion.61
  287.1 0.6 fusion.61
  288.2 0.6 fusion.61
  289.2 0.6 fusion.61
  290.3 0.6 fusion.61
  291.4 0.6 fusion.61
  294.6 0.6 fusion.61
  297.9 1.9 collective-permute-start
  299.8 2.4 collective-permute-start.1
  302.8 3.7 collective-permute-done
  306.5 3.8 collective-permute-done.1
  310.4 1.2 fusion.7
  311.6 256.9 %all-reduce.6.cloned.1.call-done = f32[256,256]{0,1:T(8,128)} async-done(((f32[256,256]{0,1:T(8,128)}), f32[256,256]{0,1:T(8,128)}) %all-reduce.6.cloned.1.call-update) | async-done | bytes 262160 | tf_op jit(solution)/shard_map/psum | solution.py:48
  568.6 1.7 select_reduce_fusion.1
  570.9 1.0 divide_select_fusion.1
  572.0 0.7 multiply_reduce_fusion.2
  573.6 12.8 %while.31 = (s32[]{:T(128)}, f32[256,256]{0,1:T(8,128)S(1)}, s32[]{:T(128)}) while((s32[]{:T(128)}, f32[256,256]{0,1:T(8,128)S(1)}, s32[]{:T(128)}) %tuple.66), condition=%wide.region_9.10_spmd, body=%wide.region_8.9_spmd.sunk | while | flops 402849792 | bytes 1835053 | solution.py:34
  574.1 0.6 fusion.67
  576.2 0.6 fusion.67
  579.4 0.6 fusion.67
  582.6 0.6 fusion.67
  585.8 0.6 fusion.67
  586.9 1.9 collective-permute-start.2
  588.9 2.4 collective-permute-start.3
  591.9 3.6 collective-permute-done.2
  595.6 3.8 collective-permute-done.3
  599.5 1.2 fusion.6
  600.7 257.0 %all-reduce.8.cloned.1.call-done = f32[256,256]{0,1:T(8,128)} async-done(((f32[256,256]{0,1:T(8,128)}), f32[256,256]{0,1:T(8,128)}) %all-reduce.8.cloned.1.call-update) | async-done | bytes 262160 | tf_op jit(solution)/shard_map/psum | solution.py:48
  857.7 1.7 select_reduce_fusion
  860.0 1.0 divide_select_fusion
  861.3 0.7 multiply_reduce_fusion.1
  862.8 12.8 %while.32 = (s32[]{:T(128)}, f32[256,256]{0,1:T(8,128)S(1)}, s32[]{:T(128)}) while((s32[]{:T(128)}, f32[256,256]{0,1:T(8,128)S(1)}, s32[]{:T(128)}) %tuple.69), condition=%wide.region_14.15_spmd, body=%wide.region_13.14_spmd.sunk | while | flops 402849792 | bytes 1835053 | solution.py:34
  863.3 0.6 fusion.73
  864.3 0.6 fusion.73
  867.5 0.6 fusion.73
  870.7 0.6 fusion.73
  873.9 0.6 fusion.73
  876.5 139.6 %psum.31 = f32[256]{0:T(256)S(1)} all-reduce(f32[256]{0:T(256)S(1)} %multiply_reduce_fusion), channel_id=1, replica_groups=mesh['rows'=64,'cols'=8] {'rows'}, use_global_device_ids=true, to_apply=%region_16.17 | all-reduce | flops 256 | bytes 2048 | tf_op jit(solution)/shard_map/psum | solution.py:65
  1016.7 1.3 copy.19
  (130 shorter events, 31.6 us)
Async XLA Ops:
  7.2 272.3 %all-reduce.4.cloned.1.call-start = ((), (), s32[]{:S(2)}) async-start(), calls=%async_computation | async-start | bytes 524288 | tf_op jit(solution)/shard_map/psum | solution.py:48
  12.2 556.3 %all-reduce.6.cloned.1.call-start = ((), (), s32[]{:S(2)}) async-start(), calls=%async_computation.1 | async-start | bytes 524288 | tf_op jit(solution)/shard_map/psum | solution.py:48
  297.9 8.6 collective-permute-start
  299.8 10.5 %collective-permute-start.1 = (bf16[2048,128]{0,1:T(8,128)(2,1)S(1)}, bf16[2048,128]{0,1:T(8,128)(2,1)S(1)}, u32[]{:S(2)}, u32[]{:S(2)}) collective-permute-start(bf16[2048,128]{0,1:T(8,128)(2,1)S(1)} %get-tuple-element.64), channel_id=1, source_target_pairs={{0,1},{1,2},{2,3},{3,4},{4,5},{5,6},{6,7},{8,9},{9,10},{10,11},{11... | collective-permute-start | bytes 1572872 | tf_op jit(solution)/shard_map/ppermute | solution.py:13
  311.6 546.1 %all-reduce.8.cloned.1.call-start = ((), (), s32[]{:S(2)}) async-start(), calls=%async_computation.2 | async-start | bytes 524288 | tf_op jit(solution)/shard_map/psum | solution.py:48
  568.6 3.4 copy-start
  586.9 8.6 collective-permute-start.2
  588.9 10.5 %collective-permute-start.3 = (bf16[2048,128]{0,1:T(8,128)(2,1)S(1)}, bf16[2048,128]{0,1:T(8,128)(2,1)S(1)}, u32[]{:S(2)}, u32[]{:S(2)}) collective-permute-start(bf16[2048,128]{0,1:T(8,128)(2,1)S(1)} %get-tuple-element.61), channel_id=1, source_target_pairs={{0,1},{1,2},{2,3},{3,4},{4,5},{5,6},{6,7},{8,9},{9,10},{10,11},{11... | collective-permute-start | bytes 1572872 | tf_op jit(solution)/shard_map/ppermute | solution.py:13
  857.7 3.4 copy-start.1
Sparse Core Ops, SparseCore 0:
  12.3 267.0 all-reduce.3
  311.7 256.8 all-reduce.5
  600.8 256.8 all-reduce.7
where the time goes:
time: 1030 us; the launch traced here: 1020 us
  waiting for transfers between devices  796 us (77%)
  blocking collectives  140 us (14%)
  matrix products  41.1 us (4%)
  between operations  19.9 us (2%)
  other arithmetic  10.7 us (1%)
    psum x3, waiting for transfers between devices, per_device(): gram = lax.psum(inner(paired, paired), 'rows')  781 us
    psum x1, blocking collectives, per_device(): squares_sum = lax.psum(jnp.sum(wide * wide, axis=0), 'rows')  140 us
    dot_general x36, matrix products, refine(): jnp.dot(iterate, square, precision=lax.Precision.HIGHEST)  21.6 us
  transfers between devices with their start and end apart: 7, of which 7 were waited for; matrix products, arithmetic and copies ran while one was open for 0% of the time, Pallas kernels for 0%

commit v1 on v0

v1 whole, which is shorter than its diff:
```python
import functools

import jax
import jax.numpy as jnp
import numpy as np
from jax import lax
from jax.experimental import pallas as pl
from jax.experimental.pallas import tpu as pltpu
from jax.sharding import PartitionSpec as P

POLAR_ITERS = 12
Y_SIZE = 4
HALF = 128
BLOCKS = 24
CHUNK = 256
F32 = jnp.float32
BF16 = jnp.bfloat16
NT = (((1,), (1,)), ((), ()))
NN = (((1,), (0,)), ((), ()))
TN = (((0,), (0,)), ((), ()))


def pair_ring(count):
    return list(range(0, count, 2)) + list(range(count - 1, 0, -2))


def moved(top, bottom):
    count = len(top)
    new_top = [top[0], bottom[0]] + top[1 : count - 1]
    new_bottom = bottom[1:] + [top[count - 1]]
    return new_top, new_bottom


def routing(count):
    ring = pair_ring(count)
    place = {pair: at for at, pair in enumerate(ring)}
    top, bottom = [(c, 0) for c in range(count)], [(c, 1) for c in range(count)]
    top_1, bottom_1 = moved(top, bottom)
    ends = [{top_1[m][0]: (0, top_1[m][1]), bottom_1[m][0]: (1, bottom_1[m][1])} for m in range(count)]
    top_2, bottom_2 = moved([(m, 0) for m in range(count)], [(m, 1) for m in range(count)])
    rows = []
    for c in range(count):
        left, right = ring[place[c] - 1], ring[(place[c] + 1) % count]
        edge_l = next(m for m in range(count) if set(ends[m]) == {left, c})
        edge_r = next(m for m in range(count) if set(ends[m]) == {right, c})
        swap_2 = int(top_2[c][0] == edge_r)
        take_l, take_r = (bottom_2[c], top_2[c]) if swap_2 else (top_2[c], bottom_2[c])
        assert (take_l[0], take_r[0]) == (edge_l, edge_r)
        flip_l, flip_r = ends[edge_l][c][0] == 0, ends[edge_r][c][0] == 1
        rows.append([
            left, right, edge_l, edge_r,
            ends[edge_l][left][1], ends[edge_l][c][1], ends[edge_r][c][1], ends[edge_r][right][1],
            int(flip_l), int(flip_r),
            int(take_l[1] == ends[edge_l][c][0]), int(take_r[1] == ends[edge_r][right][0]),
            swap_2,
        ])
    return np.array(rows, np.int32)


def dot(left, right, dims):
    return lax.dot_general(left, right, dims, preferred_element_type=F32)


def split(value):
    high = value.astype(BF16)
    return high, (value - high.astype(F32)).astype(BF16)


def fine(left, right, dims):
    if left.dtype == BF16:
        high, low = split(right)
        return dot(left, high, dims) + dot(left, low, dims)
    high, low = split(left)
    return dot(high, right, dims) + dot(low, right, dims)


def gram_kernel(left_ref, own_ref, right_ref, out_ref):
    blocks = (left_ref, own_ref, right_ref)
    at = 0
    for i in range(3):
        for j in range(i, 3):
            gram = dot(blocks[i][...], blocks[j][...], TN).astype(BF16)
            for a in range(2):
                for b in range(2):
                    out_ref[at * HALF : (at + 1) * HALF, :] = gram[a * HALF : (a + 1) * HALF, b * HALF : (b + 1) * HALF]
                    at += 1


def polar_starts(grams, signs):
    order = 2 * HALF
    row = lax.broadcasted_iota(jnp.int32, (order, order), 0)
    column = lax.broadcasted_iota(jnp.int32, (order, order), 1)
    apart = (row < HALF) != (column < HALF)
    starts = []
    for gram, sign in zip(grams, signs):
        trace_mean = jnp.sum(jnp.where(row == column, gram, 0.0)) / order + 1e-06
        upper = jnp.where(row < column, gram, 0.0) / trace_mean
        upper = jnp.where(apart, sign * upper, upper)
        initial = jnp.where(row == column, 1.0, 0.5 * (upper - upper.T))
        starts.append(initial * lax.rsqrt(jnp.sum(initial * initial)))
    return starts


def refine(iterate):
    high, low = split(iterate)
    square = dot(high, high, NT) + dot(high, low, NT) + dot(low, high, NT)
    sq_high, sq_low = split(square)
    return 1.5 * iterate - 0.5 * (dot(high, sq_high, NN) + dot(high, sq_low, NN) + dot(low, sq_high, NN))


def polars(grams, signs):
    iterates = polar_starts(grams, signs)
    for _ in range(POLAR_ITERS):
        iterates = [refine(iterate) for iterate in iterates]
    return [iterate.astype(BF16) for iterate in iterates]


def half_of(value, which):
    return jnp.where(which == 1, value[:, HALF:], value[:, :HALF])


def joined(top_left, top_right, bottom_right):
    top = jnp.concatenate([top_left, top_right], axis=1)
    bottom = jnp.concatenate([top_right.T, bottom_right], axis=1)
    return jnp.concatenate([top, bottom], axis=0)


def rounds_kernel(total_rows, pair_ref, table_ref, orient_ref, gram_ref, left_ref, own_ref, right_ref, out_ref, rms_ref, turned, held):
    pair = pair_ref[0]
    look = lambda at: table_ref[pair, at]
    sign = lambda index, flip: (1 - 2 * (index ^ flip)).astype(F32)
    left, right, edge_l, edge_r = (look(at) for at in range(4))
    half_l, half_cl, half_cr, half_r, flip_l, flip_r, take_l, take_r, swap = (look(at) for at in range(4, 13))

    def block(at):
        part = lambda k: gram_ref[(4 * at + k) * HALF : (4 * at + k + 1) * HALF, :]
        top = jnp.concatenate([part(0), part(1)], axis=1)
        bottom = jnp.concatenate([part(2), part(3)], axis=1)
        return jnp.concatenate([top, bottom], axis=0)

    g_ll, g_lc, g_lr, g_cc, g_cr, g_rr = (block(at) for at in range(6))

    r_l, r_c, r_r = polars(
        [g_ll, g_cc, g_rr],
        [sign(orient_ref[at, 0], 0) for at in (left, pair, right)],
    )
    q_l, q_cl, q_cr, q_r = half_of(r_l, half_l), half_of(r_c, half_cl), half_of(r_c, half_cr), half_of(r_r, half_r)
    q_c = jnp.concatenate([q_cl, q_cr], axis=1)
    between = lambda a, g, b: fine(a, fine(g, b, NN), TN)
    gram_l = joined(between(q_l, g_ll, q_l), between(q_l, g_lc, q_cl), between(q_cl, g_cc, q_cl))
    gram_r = joined(between(q_cr, g_cc, q_cr), between(q_cr, g_cr, q_r), between(q_r, g_rr, q_r))
    cross = jnp.concatenate([
        jnp.concatenate([between(q_l, g_lc, q_cr), between(q_l, g_lr, q_r)], axis=1),
        jnp.concatenate([between(q_cl, g_cc, q_cr), between(q_cl, g_cr, q_r)], axis=1),
    ], axis=0)

    for at in range(0, held.shape[0], CHUNK):
        rows = slice(at, at + CHUNK)
        turned[rows, :HALF] = dot(left_ref[rows, :], q_l, NN).astype(BF16)
        turned[rows, HALF : 3 * HALF] = dot(own_ref[rows, :], q_c, NN).astype(BF16)
        turned[rows, 3 * HALF :] = dot(right_ref[rows, :], q_r, NN).astype(BF16)

    e_l, e_r = polars(
        [gram_l, gram_r],
        [sign(orient_ref[edge_l, 1], flip_l), sign(orient_ref[edge_r, 1], flip_r)],
    )
    v_l, v_r = half_of(e_l, take_l), half_of(e_r, take_r)
    gram = joined(between(v_l, gram_l, v_l), between(v_l, cross, v_r), between(v_r, gram_r, v_r))

    for at in range(0, held.shape[0], CHUNK):
        rows = slice(at, at + CHUNK)
        met_l = jnp.concatenate([turned[rows, :HALF], turned[rows, HALF : 2 * HALF]], axis=1)
        met_r = jnp.concatenate([turned[rows, 2 * HALF : 3 * HALF], turned[rows, 3 * HALF :]], axis=1)
        held[rows, :HALF] = dot(met_l, v_l, NN).astype(BF16)
        held[rows, HALF:] = dot(met_r, v_r, NN).astype(BF16)

    (turn,) = polars([gram], [sign(orient_ref[pair, 2], swap)])
    turn = jnp.where(swap == 1, jnp.concatenate([turn[:, HALF:], turn[:, :HALF]], axis=1), turn)
    for at in range(0, held.shape[0], CHUNK):
        rows = slice(at, at + CHUNK)
        out_ref[rows, :] = dot(held[rows, :], turn, NN).astype(BF16)
    squares = jnp.sum(turn.astype(F32) * fine(gram, turn, NN), axis=0, keepdims=True)
    rms_ref[...] = jnp.sqrt(jnp.maximum(squares, 0.0) / total_rows)


def per_device(snapshots, orient):
    rows_axis, pairs = lax.axis_size("rows"), lax.axis_size("cols")
    z_size = rows_axis // Y_SIZE
    along_y = [[z * Y_SIZE + y for y in range(Y_SIZE)] for z in range(z_size)]
    along_z = [[z * Y_SIZE + y for z in range(z_size)] for y in range(Y_SIZE)]
    ring = pair_ring(pairs)
    forward = [(ring[at - 1], ring[at]) for at in range(pairs)]
    backward = [(target, source) for source, target in forward]

    def swapped(value, groups):
        return lax.all_to_all(value, "rows", 0, 0, axis_index_groups=groups, tiled=True)

    with jax.named_scope("neighbours"):
        left = lax.ppermute(snapshots, "cols", forward)
        right = lax.ppermute(snapshots, "cols", backward)
        turns = jnp.broadcast_to(jnp.pad(orient.reshape(1, 1, 3), ((0, 0), (0, 0), (0, HALF - 3))), (pairs, 1, HALF))
        turns = lax.all_to_all(turns, "cols", 0, 0, tiled=True).reshape(pairs, HALF)
    with jax.named_scope("gram"):
        gram = pl.pallas_call(
            gram_kernel,
            out_shape=jax.ShapeDtypeStruct((BLOCKS * HALF, HALF), BF16),
            compiler_params=pltpu.CompilerParams(vmem_limit_bytes=48 << 20),
        )(left, snapshots, right)
    with jax.named_scope("gram_sum"):
        part = swapped(gram.reshape(Y_SIZE, -1, HALF), along_y)
        part = jnp.sum(part.astype(F32), axis=0).astype(BF16)
        part = swapped(part.reshape(z_size, -1, HALF), along_z)
        part = jnp.sum(part.astype(F32), axis=0)
        part = swapped(jnp.broadcast_to(part[None], (z_size, *part.shape)), along_z).reshape(-1, HALF)
        gram = swapped(jnp.broadcast_to(part[None], (Y_SIZE, *part.shape)), along_y).reshape(-1, HALF)
    with jax.named_scope("rounds"):
        smem, vmem = pl.BlockSpec(memory_space=pltpu.SMEM), pl.BlockSpec(memory_space=pltpu.VMEM)
        rotated, column_rms = pl.pallas_call(
            functools.partial(rounds_kernel, snapshots.shape[0] * rows_axis),
            out_shape=(jax.ShapeDtypeStruct(snapshots.shape, BF16), jax.ShapeDtypeStruct((1, 2 * HALF), F32)),
            in_specs=[smem, smem, smem, vmem, vmem, vmem, vmem],
            out_specs=(vmem, vmem),
            scratch_shapes=[pltpu.VMEM((snapshots.shape[0], 4 * HALF), BF16), pltpu.VMEM(snapshots.shape, BF16)],
            compiler_params=pltpu.CompilerParams(vmem_limit_bytes=48 << 20),
        )(lax.axis_index("cols").reshape(1), jnp.asarray(routing(pairs)), turns, gram, left, snapshots, right)
    return rotated, column_rms.reshape(-1)


def solution(mesh):
    in_specs = (P("rows", "cols"), P(None, "cols"))
    out_specs = (P("rows", "cols"), P("cols"))
    return jax.shard_map(
        per_device, mesh=mesh, in_specs=in_specs, out_specs=out_specs, check_vma=False
    )
```

time: 1030 us -> 172 us (0.17)
  the two profiles are of different devices: /device:TPU:4 before, /device:TPU:32 now
where the time goes in v1:
time: 172 us; the launch traced here: 171 us
  waiting for transfers between devices  61.6 us (36%)
  blocking collectives  42.1 us (24%)
  Pallas kernels  33.3 us (19%)
  starting transfers between devices  27.1 us (16%)
  local copies, waits for them, and re-layouts  5.57 us (3%)
    all_to_all x2, blocking collectives, swapped(): lax.all_to_all(value, 'rows', 0, 0, axis_index_groups=groups, tiled=True)  42.1 us
    all_to_all x2, waiting for transfers between devices, swapped(): lax.all_to_all(value, 'rows', 0, 0, axis_index_groups=groups, tiled=True)  32.7 us
    pallas_call x1, Pallas kernels, per_device(): pl.pallas_call(functools.partial(rounds_kernel, snapshots.shape[0] * rows...  31.4 us
    ppermute x1, waiting for transfers between devices, per_device(): left = lax.ppermute(snapshots, 'cols', forward)  23 us
    all_to_all x2, starting transfers between devices, swapped(): lax.all_to_all(value, 'rows', 0, 0, axis_index_groups=groups, tiled=True)  19.1 us
    all_to_all x1, starting transfers between devices, per_device(): turns = lax.all_to_all(turns, 'cols', 0, 0, tiled=True).reshape(pairs, HALF)  6.48 us
    all_to_all x1, waiting for transfers between devices, per_device(): turns = lax.all_to_all(turns, 'cols', 0, 0, tiled=True).reshape(pairs, HALF)  5.23 us
    unnamed x16, local copies, waits for them, and re-layouts  3.7 us
  transfers between devices with their start and end apart: 5, of which 5 were waited for; matrix products, arithmetic and copies ran while one was open for 0% of the time, Pallas kernels for 0%

profile of v1, /device:TPU:32, one launch (start us, length us, event | category | flops | bytes accessed | tf_op | source)
XLA Modules:
  0.0 171.1 jit_solution(10383891061020458484)
XLA Ops:
  0.6 1.5 collective-permute-start
  2.1 0.0 collective-permute-start.1
  2.1 23.0 %collective-permute-done.left_ref = bf16[2048,256]{1,0:T(8,128)(2,1)S(1)} collective-permute-done((bf16[2048,256]{1,0:T(8,128)(2,1)}, bf16[2048,256]{1,0:T(8,128)(2,1)S(1)}, u32[]{:S(2)}, u32[]{:S(2)}) %collective-permute-start) | collective-permute-done | bytes 1048608 | tf_op jit(solution)/shard_map/neighbours/ppermute | solution.py:199
  25.1 0.0 copy-start.2
  25.1 0.6 collective-permute-done.1.right_ref
  25.8 0.0 copy-start
  25.8 1.2 copy-done
  27.0 0.0 copy-start.4
  27.0 1.8 %gram.1 = bf16[3072,128]{1,0:T(8,128)(2,1)S(1)} custom-call(bf16[2048,256]{1,0:T(8,128)(2,1)S(1)} %collective-permute-done.left_ref, bf16[2048,256]{1,0:T(8,128)(2,1)S(1)} %copy-done, bf16[2048,256]{1,0:T(8,128)(2,1)S(1)} %collective-permute-done.1.right_ref), custom_call_target="tpu_custom_call" | custom-call | tf_op jit(solution)/shard_map/gram/pallas_call | solution.py:204
  28.8 0.0 copy-done.2
  28.8 0.0 copy-done.4
  28.9 0.0 copy-start.7
  28.9 15.3 %all_to_all.25 = bf16[4,768,128]{2,1,0:T(8,128)(2,1)S(1)} all-to-all(bf16[4,768,128]{2,1,0:T(8,128)(2,1)S(1)} %bitcast.11), channel_id=1, replica_groups={{0,8,16,24},{32,40,48,56},{64,72,80,88},{96,104,112,120},{128,136,144,1..., dimensions={0} | all-to-all | bytes 1572864 | tf_op jit(solution)/shard_map/gram_sum/all_to_all | solution.py:196
  44.2 0.8 reduce_sum.21
  45.0 15.2 %all-to-all-start.2 = ((bf16[16,48,128]{2,1,0:T(8,128)(2,1)}), bf16[16,48,128]{2,1,0:T(8,128)(2,1)S(1)}, u32[]{:S(2)}, u32[]{:S(2)}) async-start(bf16[16,48,128]{2,1,0:T(8,128)(2,1)} %bitcast.5), calls=%async_computation.2 | async-start | bytes 393216 | tf_op jit(solution)/shard_map/gram_sum/all_to_all | solution.py:196
  60.2 0.0 copy-done.7
  60.3 13.4 %all-to-all-done.2 = bf16[16,48,128]{2,1,0:T(8,128)(2,1)S(1)} async-done(((bf16[16,48,128]{2,1,0:T(8,128)(2,1)}), bf16[16,48,128]{2,1,0:T(8,128)(2,1)S(1)}, u32[]{:S(2)}, u32[]{:S(2)}) %all-to-all-start.2) | async-done | bytes 196640 | tf_op jit(solution)/shard_map/gram_sum/all_to_all | solution.py:196
  73.7 0.6 broadcast_in_dim.21
  74.2 6.5 %all-to-all-start = ((s32[8,1,128]{2,1,0:T(1,128)}), s32[8,1,128]{2,1,0:T(1,128)S(1)}, u32[]{:S(2)}, u32[]{:S(2)}) async-start(s32[8,1,128]{2,1,0:T(1,128)} %broadcast_in_dim.21), calls=%async_computation | async-start | bytes 8192 | tf_op jit(solution)/shard_map/neighbours/all_to_all | solution.py:202
  80.7 5.2 %all-to-all-done = s32[8,1,128]{2,1,0:T(1,128)S(1)} async-done(((s32[8,1,128]{2,1,0:T(1,128)}), s32[8,1,128]{2,1,0:T(1,128)S(1)}, u32[]{:S(2)}, u32[]{:S(2)}) %all-to-all-start) | async-done | bytes 4128 | tf_op jit(solution)/shard_map/neighbours/all_to_all | solution.py:202
  86.0 26.8 %all_to_all.26 = f32[16,48,128]{2,1,0:T(8,128)S(1)} all-to-all(f32[16,48,128]{2,1,0:T(8,128)S(1)} %broadcast_in_dim.22), channel_id=1, replica_groups={{0,32,64,96,128,160,192,224,256,288,320,352,384,416,448,480},{8,40,72,1..., dimensions={0} | all-to-all | bytes 786432 | tf_op jit(solution)/shard_map/gram_sum/all_to_all | solution.py:196
  112.8 1.3 broadcast_in_dim.24
  114.1 0.0 copy-start.1
  114.1 0.0 copy-start.6
  114.1 3.9 %all-to-all-start.4 = ((f32[4,768,128]{2,1,0:T(8,128)}), f32[4,768,128]{2,1,0:T(8,128)S(1)}, u32[]{:S(2)}, u32[]{:S(2)}) async-start(f32[4,768,128]{2,1,0:T(8,128)} %broadcast_in_dim.24), calls=%async_computation.4 | async-start | bytes 3145728 | tf_op jit(solution)/shard_map/gram_sum/all_to_all | solution.py:196
  118.0 19.3 %all-to-all-done.4 = f32[4,768,128]{2,1,0:T(8,128)S(1)} async-done(((f32[4,768,128]{2,1,0:T(8,128)}), f32[4,768,128]{2,1,0:T(8,128)S(1)}, u32[]{:S(2)}, u32[]{:S(2)}) %all-to-all-start.4) | async-done | bytes 1572896 | tf_op jit(solution)/shard_map/gram_sum/all_to_all | solution.py:196
  137.3 0.0 copy-done.1
  137.3 0.0 copy-done.6
  137.3 0.0 copy-start.3
  137.3 1.2 copy-done.3
  138.5 0.0 copy-start.5
  138.5 1.2 copy-done.5
  139.7 31.4 %rounds.1 = (bf16[2048,256]{1,0:T(8,128)(2,1)}, f32[1,256]{1,0:T(1,128)}) custom-call(s32[1]{0:T(128)} %bitcast.pair_ref, s32[8,13]{1,0:T(8,128)S(1)} %copy-done.6, s32[8,128]{1,0:T(8,128)S(1)} %bitcast.12, f32[3072,128]{1,0:T(8,128)S(1)} %bitcast.10, bf16[2048,256]{1,0:T(8,128)(2,1)S(1)} %copy-done.3, bf16[2048,256]{1,0:T(8,128)(2,1)S(1)} %copy-done.1, ...), custom_call_target="tpu_custom_call" | custom-call | tf_op jit(solution)/shard_map/rounds/pallas_call | solution.py:218
  (3 shorter events, 0.1 us)
Async XLA Ops:
  0.6 24.5 %collective-permute-start = (bf16[2048,256]{1,0:T(8,128)(2,1)}, bf16[2048,256]{1,0:T(8,128)(2,1)S(1)}, u32[]{:S(2)}, u32[]{:S(2)}) collective-permute-start(bf16[2048,256]{1,0:T(8,128)(2,1)} %own_ref.3), channel_id=1, source_target_pairs={{1,0},{0,2},{2,4},{4,6},{6,7},{7,5},{5,3},{3,1},{9,8},{8,10},{10,1... | collective-permute-start | bytes 3145736 | tf_op jit(solution)/shard_map/neighbours/ppermute | solution.py:199
  2.1 23.6 %collective-permute-start.1 = (bf16[2048,256]{1,0:T(8,128)(2,1)}, bf16[2048,256]{1,0:T(8,128)(2,1)S(1)}, u32[]{:S(2)}, u32[]{:S(2)}) collective-permute-start(bf16[2048,256]{1,0:T(8,128)(2,1)} %own_ref.3), channel_id=1, source_target_pairs={{0,1},{2,0},{4,2},{6,4},{7,6},{5,7},{3,5},{1,3},{8,9},{10,8},{12,1... | collective-permute-start | bytes 3145736 | tf_op jit(solution)/shard_map/neighbours/ppermute | solution.py:200
  25.1 3.7 %copy-start.2 = (bf16[2048,256]{1,0:T(8,128)(2,1)}, bf16[2048,256]{1,0:T(8,128)(2,1)S(1)}, u32[]{:S(2)}) copy-start(bf16[2048,256]{1,0:T(8,128)(2,1)S(1)} %collective-permute-done.left_ref) | copy-start | bytes 3145732
  25.8 1.2 copy-start
  27.0 1.9 %copy-start.4 = (bf16[2048,256]{1,0:T(8,128)(2,1)}, bf16[2048,256]{1,0:T(8,128)(2,1)S(1)}, u32[]{:S(2)}) copy-start(bf16[2048,256]{1,0:T(8,128)(2,1)S(1)} %collective-permute-done.1.right_ref) | copy-start | bytes 3145732
  28.9 31.4 %copy-start.7 = (s32[3,1]{0,1:T(1,128)S(1)}, s32[3,1]{0,1:T(1,128)}, u32[]{:S(2)}) copy-start(s32[3,1]{0,1:T(1,128)} %param.4) | copy-start | bytes 40
  45.0 28.6 %all-to-all-start.2 = ((bf16[16,48,128]{2,1,0:T(8,128)(2,1)}), bf16[16,48,128]{2,1,0:T(8,128)(2,1)S(1)}, u32[]{:S(2)}, u32[]{:S(2)}) async-start(bf16[16,48,128]{2,1,0:T(8,128)(2,1)} %bitcast.5), calls=%async_computation.2 | async-start | bytes 393216 | tf_op jit(solution)/shard_map/gram_sum/all_to_all | solution.py:196
  74.2 11.7 %all-to-all-start = ((s32[8,1,128]{2,1,0:T(1,128)}), s32[8,1,128]{2,1,0:T(1,128)S(1)}, u32[]{:S(2)}, u32[]{:S(2)}) async-start(s32[8,1,128]{2,1,0:T(1,128)} %broadcast_in_dim.21), calls=%async_computation | async-start | bytes 8192 | tf_op jit(solution)/shard_map/neighbours/all_to_all | solution.py:202
  114.1 23.2 %copy-start.1 = (bf16[2048,256]{1,0:T(8,128)(2,1)S(1)}, bf16[2048,256]{1,0:T(8,128)(2,1)}, u32[]{:S(2)}) copy-start(bf16[2048,256]{1,0:T(8,128)(2,1)} %own_ref.3) | copy-start | bytes 3145732
  114.1 23.2 %copy-start.6 = (s32[8,13]{1,0:T(8,128)S(1)}, s32[8,13]{1,0:T(8,128)}, u32[]{:S(2)}) copy-start(s32[8,13]{1,0:T(8,128)} %constant.12.clone.table_ref) | copy-start | bytes 1252
  114.1 23.2 %all-to-all-start.4 = ((f32[4,768,128]{2,1,0:T(8,128)}), f32[4,768,128]{2,1,0:T(8,128)S(1)}, u32[]{:S(2)}, u32[]{:S(2)}) async-start(f32[4,768,128]{2,1,0:T(8,128)} %broadcast_in_dim.24), calls=%async_computation.4 | async-start | bytes 3145728 | tf_op jit(solution)/shard_map/gram_sum/all_to_all | solution.py:196
  137.3 1.2 copy-start.3
  138.5 1.2 copy-start.5

commit v2 on v1

v2 whole, which is shorter than its diff:
```python
import functools

import jax
import jax.numpy as jnp
import numpy as np
from jax import lax
from jax.experimental import pallas as pl
from jax.experimental.pallas import tpu as pltpu
from jax.sharding import PartitionSpec as P

POLAR_ITERS = 12
Y_SIZE = 4
HALF = 128
CHUNK = 256
F32 = jnp.float32
BF16 = jnp.bfloat16
NT = (((1,), (1,)), ((), ()))
NN = (((1,), (0,)), ((), ()))
TN = (((0,), (0,)), ((), ()))


def pair_ring(count):
    return list(range(0, count, 2)) + list(range(count - 1, 0, -2))


def moved(top, bottom):
    count = len(top)
    new_top = [top[0], bottom[0]] + top[1 : count - 1]
    new_bottom = bottom[1:] + [top[count - 1]]
    return new_top, new_bottom


def routing(count):
    ring = pair_ring(count)
    place = {pair: at for at, pair in enumerate(ring)}
    top, bottom = [(c, 0) for c in range(count)], [(c, 1) for c in range(count)]
    top_1, bottom_1 = moved(top, bottom)
    ends = [{top_1[m][0]: (0, top_1[m][1]), bottom_1[m][0]: (1, bottom_1[m][1])} for m in range(count)]
    top_2, bottom_2 = moved([(m, 0) for m in range(count)], [(m, 1) for m in range(count)])
    rows = []
    for c in range(count):
        left, right = ring[place[c] - 1], ring[(place[c] + 1) % count]
        edge_l = next(m for m in range(count) if set(ends[m]) == {left, c})
        edge_r = next(m for m in range(count) if set(ends[m]) == {right, c})
        swap_2 = int(top_2[c][0] == edge_r)
        take_l, take_r = (bottom_2[c], top_2[c]) if swap_2 else (top_2[c], bottom_2[c])
        assert (take_l[0], take_r[0]) == (edge_l, edge_r)
        flip_l, flip_r = ends[edge_l][c][0] == 0, ends[edge_r][c][0] == 1
        rows.append([
            left, right, edge_l, edge_r,
            ends[edge_l][left][1], ends[edge_l][c][1], ends[edge_r][c][1], ends[edge_r][right][1],
            int(flip_l), int(flip_r),
            int(take_l[1] == ends[edge_l][c][0]), int(take_r[1] == ends[edge_r][right][0]),
            swap_2,
        ])
    return np.array(rows, np.int32)


def dot(left, right, dims):
    return lax.dot_general(left, right, dims, preferred_element_type=F32)


def split(value):
    high = value.astype(BF16)
    return high, (value - high.astype(F32)).astype(BF16)


def fine(left, right, dims):
    if left.dtype == BF16:
        high, low = split(right)
        return dot(left, high, dims) + dot(left, low, dims)
    high, low = split(left)
    return dot(high, right, dims) + dot(low, right, dims)


def triangle(shape):
    return lax.broadcasted_iota(jnp.int32, shape, 0), lax.broadcasted_iota(jnp.int32, shape, 1)


def own_gram_kernel(own_ref, out_ref):
    total = dot(own_ref[...], own_ref[...], TN)
    first, apart, second = total[:HALF, :HALF], total[:HALF, HALF:], total[HALF:, HALF:]
    row, column = triangle(first.shape)
    diagonal = jnp.sum(jnp.where(row == column, second, 0.0), axis=0, keepdims=True)
    packed = jnp.concatenate([jnp.where(row <= column, first, second), apart], axis=0)
    pieces, rows = out_ref.shape[0], out_ref.shape[1] - 8
    for at in range(pieces):
        out_ref[at, :rows] = packed[at * rows : (at + 1) * rows]
        out_ref[at, rows:] = jnp.broadcast_to(diagonal, (8, HALF))


def cross_gram_kernel(left_ref, own_ref, right_ref, gram_ref, out_ref):
    per_device, piece = 3 * HALF, gram_ref.shape[1] - 8
    total = jnp.sum(gram_ref[...], axis=0)
    high = total.astype(BF16).astype(F32)
    low = total - high
    extra = jnp.concatenate([high[:piece], low[:piece], high[piece:], low[piece:]], axis=0).astype(BF16)
    for at in range(out_ref.shape[0]):
        out_ref[at, per_device:] = extra
    pairs = (left_ref, own_ref), (own_ref, right_ref), (left_ref, right_ref)
    totals = [dot(one[...], two[...], TN) for one, two in pairs]
    for at in range(12):
        a, b, row = at // 2 % 2, at % 2, at % 3 * HALF
        block = totals[at // 4][a * HALF : (a + 1) * HALF, b * HALF : (b + 1) * HALF]
        out_ref[at // 3, row : row + HALF] = block.astype(BF16)


def summed_y_kernel(both_ref, out_ref, diagonal_ref):
    count, per_device = out_ref.shape[0], 3 * HALF
    step = per_device // count
    piece = out_ref.shape[1] - step
    cross = sum(both_ref[y, :per_device].astype(F32) for y in range(Y_SIZE))
    extra = sum(both_ref[y, per_device:].astype(F32) for y in range(Y_SIZE))
    gram = extra[:piece] + extra[piece : 2 * piece]
    diagonal_ref[...] = extra[2 * piece : 2 * piece + 8] + extra[2 * piece + 8 :]
    for at in range(count):
        out_ref[at, :step] = cross[at * step : (at + 1) * step]
        out_ref[at, step:] = gram


def summed_z_kernel(both_ref, out_ref, gram_ref):
    count, step = out_ref.shape[:2]
    piece = both_ref.shape[1] - step
    cross = jnp.sum(both_ref[:, :step], axis=0)
    for at in range(count):
        out_ref[at] = cross
        gram_ref[at * piece : (at + 1) * piece] = both_ref[at, step:]


def unpacked(packed_ref, diagonal):
    both, apart = packed_ref[:HALF, :], packed_ref[HALF:, :]
    row, column = triangle(both.shape)
    turned = both.T
    first = jnp.where(row <= column, both, turned)
    second = jnp.where(row == column, diagonal, jnp.where(row > column, both, turned))
    return joined(first, apart, second)


def block_of(part):
    top = jnp.concatenate([part(0), part(1)], axis=1)
    bottom = jnp.concatenate([part(2), part(3)], axis=1)
    return jnp.concatenate([top, bottom], axis=0)


def polar_starts(grams, signs):
    order = 2 * HALF
    row = lax.broadcasted_iota(jnp.int32, (order, order), 0)
    column = lax.broadcasted_iota(jnp.int32, (order, order), 1)
    apart = (row < HALF) != (column < HALF)
    starts = []
    for gram, sign in zip(grams, signs):
        trace_mean = jnp.sum(jnp.where(row == column, gram, 0.0)) / order + 1e-06
        upper = jnp.where(row < column, gram, 0.0) / trace_mean
        upper = jnp.where(apart, sign * upper, upper)
        initial = jnp.where(row == column, 1.0, 0.5 * (upper - upper.T))
        starts.append(initial * lax.rsqrt(jnp.sum(initial * initial)))
    return starts


def refine(iterate):
    high, low = split(iterate)
    square = dot(high, high, NT) + dot(high, low, NT) + dot(low, high, NT)
    sq_high, sq_low = split(square)
    return 1.5 * iterate - 0.5 * (dot(sq_high, high, NN) + dot(sq_low, high, NN) + dot(sq_high, low, NN))


def polars(grams, signs):
    iterates = polar_starts(grams, signs)
    for _ in range(POLAR_ITERS):
        iterates = [refine(iterate) for iterate in iterates]
    return [iterate.astype(BF16) for iterate in iterates]


def half_of(value, which):
    return jnp.where(which == 1, value[:, HALF:], value[:, :HALF])


def joined(top_left, top_right, bottom_right):
    top = jnp.concatenate([top_left, top_right], axis=1)
    bottom = jnp.concatenate([top_right.T, bottom_right], axis=1)
    return jnp.concatenate([top, bottom], axis=0)


def between(one, gram, two):
    return fine(one, fine(gram, two, NN), TN)


def sign_of(flag, flip):
    return (1 - 2 * (flag ^ flip)).astype(F32)


def first_round_kernel(pair_ref, table_ref, orient_ref, gram_ref, diagonal_ref, back_ref, ahead_ref, mid_ref):
    pair = pair_ref[0]
    gram = unpacked(gram_ref, diagonal_ref[:1, :])
    (turn,) = polars([gram], [sign_of(orient_ref[0], 0)])
    q_cl, q_cr = half_of(turn, table_ref[pair, 5]), half_of(turn, table_ref[pair, 6])
    for ref, q in ((back_ref, q_cl), (ahead_ref, q_cr)):
        high, low = split(between(q, gram, q))
        ref[: 2 * HALF, :] = q
        ref[2 * HALF : 3 * HALF, :] = high
        ref[3 * HALF :, :] = low
    mid_ref[...] = between(q_cl, gram, q_cr)


def rounds_kernel(
    total_rows, pair_ref, table_ref, orient_ref, below_ref, above_ref,
    *rest,
):
    sources, (out_ref, rms_ref), (*kept, held, arrived) = rest[:9], rest[9:11], rest[11:]
    copies = [pltpu.make_async_copy(source, place, arrived.at[at]) for at, (source, place) in enumerate(zip(sources, kept))]
    for copy in copies:
        copy.start()
    gram_ref, from_left_ref, back_ref, ahead_ref, from_right_ref, mid_ref, left_ref, own_ref, right_ref = kept
    pair = pair_ref[0]
    look = lambda at: table_ref[pair, at]
    edge_l, edge_r, flip_l, flip_r, take_l, take_r, swap = (look(at) for at in (2, 3, 8, 9, 10, 11, 12))
    of_edge = lambda edge: jnp.where(edge < pair, below_ref[1], jnp.where(edge > pair, above_ref[1], orient_ref[1]))

    for copy in copies[:6]:
        copy.wait()
    g_lc, g_cr, g_lr = (block_of(lambda k: gram_ref[(4 * at + k) * HALF : (4 * at + k + 1) * HALF, :]) for at in range(3))
    q_l, q_cl, q_cr, q_r = (ref[: 2 * HALF, :] for ref in (from_left_ref, back_ref, ahead_ref, from_right_ref))
    d_l, d_cl, d_cr, d_r = (
        ref[2 * HALF : 3 * HALF, :].astype(F32) + ref[3 * HALF :, :].astype(F32)
        for ref in (from_left_ref, back_ref, ahead_ref, from_right_ref)
    )
    gram_l = joined(d_l, between(q_l, g_lc, q_cl), d_cl)
    gram_r = joined(d_cr, between(q_cr, g_cr, q_r), d_r)
    cross = jnp.concatenate([
        jnp.concatenate([between(q_l, g_lc, q_cr), between(q_l, g_lr, q_r)], axis=1),
        jnp.concatenate([mid_ref[...], between(q_cl, g_cr, q_r)], axis=1),
    ], axis=0)

    e_l, e_r = polars([gram_l, gram_r], [sign_of(of_edge(edge_l), flip_l), sign_of(of_edge(edge_r), flip_r)])
    v_l, v_r = half_of(e_l, take_l), half_of(e_r, take_r)
    gram = joined(between(v_l, gram_l, v_l), between(v_l, cross, v_r), between(v_r, gram_r, v_r))

    for copy in copies[6:]:
        copy.wait()
    q_c = jnp.concatenate([q_cl, q_cr], axis=1)
    for at in range(0, held.shape[0], CHUNK):
        rows = slice(at, at + CHUNK)
        turned_l = dot(left_ref[rows, :], q_l, NN).astype(BF16)
        turned_c = dot(own_ref[rows, :], q_c, NN).astype(BF16)
        turned_r = dot(right_ref[rows, :], q_r, NN).astype(BF16)
        met_l = jnp.concatenate([turned_l, turned_c[:, :HALF]], axis=1)
        met_r = jnp.concatenate([turned_c[:, HALF:], turned_r], axis=1)
        held[rows, :HALF] = dot(met_l, v_l, NN).astype(BF16)
        held[rows, HALF:] = dot(met_r, v_r, NN).astype(BF16)

    (turn,) = polars([gram], [sign_of(orient_ref[2], swap)])
    turn = jnp.where(swap == 1, jnp.concatenate([turn[:, HALF:], turn[:, :HALF]], axis=1), turn)
    for at in range(0, held.shape[0], CHUNK):
        rows = slice(at, at + CHUNK)
        out_ref[rows, :] = dot(held[rows, :], turn, NN).astype(BF16)
    squares = jnp.sum(turn.astype(F32) * fine(gram, turn, NN), axis=0, keepdims=True)
    rms_ref[...] = jnp.sqrt(jnp.maximum(squares, 0.0) / total_rows)


def call(kernel, outs, spaces, operands, micros, scratch=(), megabytes=8):
    space = {"s": pltpu.SMEM, "v": pltpu.VMEM, "a": pl.ANY}
    return pl.pallas_call(
        kernel,
        out_shape=outs,
        in_specs=[pl.BlockSpec(memory_space=space[name]) for name in spaces],
        out_specs=jax.tree.map(lambda _: pl.BlockSpec(memory_space=pltpu.VMEM), outs),
        scratch_shapes=scratch,
        compiler_params=pltpu.CompilerParams(vmem_limit_bytes=megabytes << 20),
        cost_estimate=pl.CostEstimate(flops=micros * 10**9, bytes_accessed=0, transcendentals=0),
    )(*operands)


def per_device(snapshots, orient):
    rows_axis, pairs = lax.axis_size("rows"), lax.axis_size("cols")
    z_size = rows_axis // Y_SIZE
    along_y = [[z * Y_SIZE + y for y in range(Y_SIZE)] for z in range(z_size)]
    along_z = [[z * Y_SIZE + y for z in range(z_size)] for y in range(Y_SIZE)]
    ring = pair_ring(pairs)
    forward = [(ring[at - 1], ring[at]) for at in range(pairs)]
    backward = [(target, source) for source, target in forward]
    shape = jax.ShapeDtypeStruct
    height = snapshots.shape[0]
    pair = lax.axis_index("cols").reshape(1)
    table = jnp.asarray(routing(pairs))
    orient = orient.reshape(-1)

    def swapped(value, count, groups):
        return lax.all_to_all(value.reshape(count, -1, HALF), "rows", 0, 0, axis_index_groups=groups, tiled=True)

    def gathered(value, count, groups):
        return swapped(jnp.broadcast_to(value[None], (count, *value.shape)), count, groups).reshape(-1, HALF)

    with jax.named_scope("neighbours"):
        left = lax.ppermute(snapshots, "cols", forward)
        right = lax.ppermute(snapshots, "cols", backward)
    with jax.named_scope("own_gram"):
        piece, step = 2 * HALF // z_size, 3 * HALF // z_size
        gram = call(
            own_gram_kernel, shape((z_size, piece + 8, HALF), F32), "v", (snapshots,), 1
        )
        gram = swapped(gram, z_size, along_z)
    left, right, gram = lax.optimization_barrier((left, right, gram))
    with jax.named_scope("sum_y"):
        both = call(
            cross_gram_kernel, shape((Y_SIZE, 3 * HALF + 2 * (piece + 8), HALF), BF16), "vvvv",
            (left, snapshots, right, gram), 2,
        )
        both = swapped(both, Y_SIZE, along_y)
        both, diagonal = call(
            summed_y_kernel, (shape((z_size, step + piece, HALF), F32), shape((8, HALF), F32)), "v", (both,), 1
        )
    both, orient = lax.optimization_barrier((both, orient))
    with jax.named_scope("neighbours"):
        below = lax.ppermute(orient, "cols", [(c - 1, c) for c in range(1, pairs)])
        above = lax.ppermute(orient, "cols", [(c, c - 1) for c in range(1, pairs)])
    with jax.named_scope("sum_z"):
        both = swapped(both, z_size, along_z)
        cross, gram = call(
            summed_z_kernel, (shape((z_size, step, HALF), F32), shape((2 * HALF, HALF), F32)), "v", (both,), 1
        )
    cross, gram, below, above = lax.optimization_barrier((cross, gram, below, above))
    with jax.named_scope("gather_z"):
        cross = swapped(cross, z_size, along_z).reshape(-1, HALF)
    with jax.named_scope("first_round"):
        sent = shape((4 * HALF, HALF), BF16)
        back, ahead, mid = call(
            first_round_kernel, (sent, sent, shape((HALF, HALF), F32)), "sssvv",
            (pair, table, orient, gram, diagonal), 9,
        )
    cross, back, ahead, mid = lax.optimization_barrier((cross, back, ahead, mid))
    with jax.named_scope("gather_y"):
        cross = gathered(cross, Y_SIZE, along_y)
    with jax.named_scope("neighbours"):
        from_left = lax.ppermute(ahead, "cols", forward)
        from_right = lax.ppermute(back, "cols", backward)
    with jax.named_scope("rounds"):
        operands = (cross, from_left, back, ahead, from_right, mid, left, snapshots, right)
        rotated, column_rms = call(
            functools.partial(rounds_kernel, height * rows_axis),
            (shape(snapshots.shape, BF16), shape((1, 2 * HALF), F32)),
            "sssss" + "a" * len(operands),
            (pair, table, orient, below, above, *operands),
            21,
            [pltpu.VMEM(value.shape, value.dtype) for value in operands]
            + [pltpu.VMEM(snapshots.shape, BF16), pltpu.SemaphoreType.DMA((len(operands),))],
            megabytes=52,
        )
    return rotated, column_rms.reshape(-1)


def solution(mesh):
    in_specs = (P("rows", "cols"), P(None, "cols"))
    out_specs = (P("rows", "cols"), P("cols"))
    return jax.shard_map(
        per_device, mesh=mesh, in_specs=in_specs, out_specs=out_specs, check_vma=False
    )
```

time: 172 us -> 136 us (0.79)
  waiting for transfers between devices: 61.6 us -> 29 us
  local copies, waits for them, and re-layouts: 5.57 us -> 3.12 us
    ppermute x1, waiting for transfers between devices: 23 us -> 0.01 us  [per_device(): left = lax.ppermute(snapshots, 'cols', forward)]
    all_to_all x3, waiting for transfers between devices: 37.9 us -> 24 us  [swapped(): lax.all_to_all(value.reshape(count, -1, HALF), 'rows', 0, 0, axis_index_g...]
    all_to_all x3, starting transfers between devices: 25.6 us -> 18 us  [swapped(): lax.all_to_all(value.reshape(count, -1, HALF), 'rows', 0, 0, axis_index_g...]
    ppermute x0 -> x4, starting transfers between devices: none -> 5.82 us  [the longest x1 3.03 us: per_device(): below = lax.ppermute(orient, 'cols', [(c - 1, c) for c in range(1, pairs)])]
    ppermute x0 -> x4, waiting for transfers between devices: none -> 4.97 us  [the longest x1 2.52 us: per_device(): from_left = lax.ppermute(ahead, 'cols', forward)]
    unnamed x16 -> x10, local copies, waits for them, and re-layouts: 3.7 us -> 2.19 us
    pallas_call x2 -> x6, Pallas kernels: 33.3 us -> 33.5 us  [call(): pl.pallas_call(kernel, out_shape=outs, in_specs=[pl.BlockSpec(memory_spac...]
  transfers between devices with their start and end apart: 5 -> 9, of which waited for: 5 -> 5; matrix products, arithmetic and copies ran while one was open for 0% -> 0% of each run, Pallas kernels for 0% -> 7%
where the time goes in v2:
time: 136 us; the launch traced here: 135 us
  blocking collectives  42.7 us (31%)
  Pallas kernels  33.5 us (25%)
  waiting for transfers between devices  29 us (21%)
  starting transfers between devices  25.8 us (19%)
  local copies, waits for them, and re-layouts  3.12 us (2%)
    all_to_all x2, blocking collectives, swapped(): lax.all_to_all(value.reshape(count, -1, HALF), 'rows', 0, 0, axis_index_g...  42.7 us
    pallas_call x6, Pallas kernels, call(): pl.pallas_call(kernel, out_shape=outs, in_specs=[pl.BlockSpec(memory_spac...  33.5 us
    all_to_all x3, waiting for transfers between devices, swapped(): lax.all_to_all(value.reshape(count, -1, HALF), 'rows', 0, 0, axis_index_g...  24 us
    all_to_all x3, starting transfers between devices, swapped(): lax.all_to_all(value.reshape(count, -1, HALF), 'rows', 0, 0, axis_index_g...  18 us
    ppermute x1, starting transfers between devices, per_device(): below = lax.ppermute(orient, 'cols', [(c - 1, c) for c in range(1, pairs)])  3.03 us
  transfers between devices with their start and end apart: 9, of which 5 were waited for; matrix products, arithmetic and copies ran while one was open for 0% of the time, Pallas kernels for 7%

profile of v2, /device:TPU:32, one launch (start us, length us, event | category | flops | bytes accessed | tf_op | source)
XLA Modules:
  0.0 135.0 jit_solution(8019740114024832434)
XLA Ops:
  0.6 0.0 collective-permute-start.1
  0.7 2.0 %collective-permute-start = (bf16[2048,256]{1,0:T(8,128)(2,1)}, bf16[2048,256]{1,0:T(8,128)(2,1)S(1)}, u32[]{:S(2)}, u32[]{:S(2)}) collective-permute-start(bf16[2048,256]{1,0:T(8,128)(2,1)} %rest_7_.1), channel_id=1, source_target_pairs={{1,0},{0,2},{2,4},{4,6},{6,7},{7,5},{5,3},{3,1},{9,8},{8,10},{10,1... | collective-permute-start | bytes 3145736 | tf_op jit(solution)/shard_map/neighbours/ppermute | solution.py:294
  2.7 0.0 copy-start
  2.7 1.3 copy-done
  3.9 0.5 own_gram.1
  4.4 30.8 %all_to_all.25.gram_ref = f32[16,24,128]{2,1,0:T(8,128)S(1)} all-to-all(f32[16,24,128]{2,1,0:T(8,128)S(1)} %own_gram.1), channel_id=1, replica_groups={{0,32,64,96,128,160,192,224,256,288,320,352,384,416,448,480},{8,40,72,1..., dimensions={0} | all-to-all | bytes 393216 | tf_op jit(solution)/shard_map/own_gram/all_to_all | solution.py:288
  35.2 0.0 collective-permute-done.1.right_ref.rest_8_
  35.2 0.0 copy-start.1
  35.2 0.0 collective-permute-done.left_ref.rest_6_
  35.2 0.0 copy-start.2
  35.2 1.0 sum_y.2
  36.3 0.0 copy-done.1
  36.3 0.3 copy-done.2
  36.6 11.9 %all_to_all.26.both_ref = bf16[4,432,128]{2,1,0:T(8,128)(2,1)S(1)} all-to-all(bf16[4,432,128]{2,1,0:T(8,128)(2,1)S(1)} %sum_y.2), channel_id=1, replica_groups={{0,8,16,24},{32,40,48,56},{64,72,80,88},{96,104,112,120},{128,136,144,1..., dimensions={0} | all-to-all | bytes 884736 | tf_op jit(solution)/shard_map/sum_y/all_to_all | solution.py:288
  48.5 0.8 sum_y.3
  49.2 7.8 %all-to-all-start.2 = ((f32[16,40,128]{2,1,0:T(8,128)}), f32[16,40,128]{2,1,0:T(8,128)S(1)}, u32[]{:S(2)}, u32[]{:S(2)}) async-start(f32[16,40,128]{2,1,0:T(8,128)} %get-tuple-element.29), calls=%async_computation.2 | async-start | bytes 655360 | tf_op jit(solution)/shard_map/sum_z/all_to_all | solution.py:288
  57.0 0.0 copy-start.3
  57.0 0.6 copy-done.3
  57.7 1.3 collective-permute-start.3
  58.9 3.0 %collective-permute-start.2 = (s32[3]{0:T(128)S(1)}, s32[3]{0:T(128)S(1)}, u32[]{:S(2)}, u32[]{:S(2)}) collective-permute-start(s32[3]{0:T(128)S(1)} %bitcast.7), channel_id=1, source_target_pairs={{0,1},{1,2},{2,3},{3,4},{4,5},{5,6},{6,7},{8,9},{9,10},{10,11},{11... | collective-permute-start | bytes 44 | tf_op jit(solution)/shard_map/neighbours/ppermute | solution.py:314
  62.0 13.9 %all-to-all-done.2.both_ref = f32[16,40,128]{2,1,0:T(8,128)S(1)} async-done(((f32[16,40,128]{2,1,0:T(8,128)}), f32[16,40,128]{2,1,0:T(8,128)S(1)}, u32[]{:S(2)}, u32[]{:S(2)}) %all-to-all-start.2) | async-done | bytes 327712 | tf_op jit(solution)/shard_map/sum_z/all_to_all | solution.py:288
  75.9 0.7 sum_z.1
  76.6 0.0 collective-permute-done.3.above_ref
  76.6 0.0 collective-permute-done.2.below_ref
  76.6 0.0 copy-start.4
  76.6 6.7 %all-to-all-start.3 = ((f32[16,24,128]{2,1,0:T(8,128)}), f32[16,24,128]{2,1,0:T(8,128)S(1)}, u32[]{:S(2)}, u32[]{:S(2)}) async-start(f32[16,24,128]{2,1,0:T(8,128)} %get-tuple-element.34), calls=%async_computation.3 | async-start | bytes 393216 | tf_op jit(solution)/shard_map/gather_z/all_to_all | solution.py:288
  83.4 0.0 copy-done.4
  83.4 8.9 %first_round.1 = (bf16[512,128]{1,0:T(8,128)(2,1)S(1)}, bf16[512,128]{1,0:T(8,128)(2,1)S(1)}, f32[128,128]{1,0:T(8,128)S(1)}) custom-call(s32[1]{0:T(128)} %bitcast.pair_ref, s32[8,13]{1,0:T(8,128)S(1)} %copy-done.4, s32[3]{0:T(128)S(1)} %bitcast.8, f32[256,128]{1,0:T(8,128)S(1)} %get-tuple-element.35.gram_ref, f32[8,128]{1,0:T(8,128)S(1)} %get-tuple-element.36.diagonal_ref), custom_call_target="tpu_custom_call" | custom-call | flops 8999999488 | tf_op jit(solution)/shard_map/first_round/pallas_call | solution.py:262
  92.3 7.1 %all-to-all-done.3 = f32[16,24,128]{2,1,0:T(8,128)S(1)} async-done(((f32[16,24,128]{2,1,0:T(8,128)}), f32[16,24,128]{2,1,0:T(8,128)S(1)}, u32[]{:S(2)}, u32[]{:S(2)}) %all-to-all-start.3) | async-done | bytes 196640 | tf_op jit(solution)/shard_map/gather_z/all_to_all | solution.py:288
  99.4 0.9 broadcast_in_dim.2
  100.3 3.5 %all-to-all-start.4 = ((f32[4,384,128]{2,1,0:T(8,128)}), f32[4,384,128]{2,1,0:T(8,128)S(1)}, u32[]{:S(2)}, u32[]{:S(2)}) async-start(f32[4,384,128]{2,1,0:T(8,128)} %broadcast_in_dim.2), calls=%async_computation.4 | async-start | bytes 1572864 | tf_op jit(solution)/shard_map/gather_y/all_to_all | solution.py:288
  103.8 1.5 %collective-permute-start.4 = (bf16[512,128]{1,0:T(8,128)(2,1)S(1)}, bf16[512,128]{1,0:T(8,128)(2,1)S(1)}, u32[]{:S(2)}, u32[]{:S(2)}) collective-permute-start(bf16[512,128]{1,0:T(8,128)(2,1)S(1)} %get-tuple-element.41.rest_3_), channel_id=1, source_target_pairs={{1,0},{0,2},{2,4},{4,6},{6,7},{7,5},{5,3},{3,1},{9,8},{8,10},{10,1... | collective-permute-start | bytes 393224 | tf_op jit(solution)/shard_map/neighbours/ppermute | solution.py:334
  105.3 0.0 collective-permute-start.5
  105.3 2.5 %collective-permute-done.4.rest_1_ = bf16[512,128]{1,0:T(8,128)(2,1)S(1)} collective-permute-done((bf16[512,128]{1,0:T(8,128)(2,1)S(1)}, bf16[512,128]{1,0:T(8,128)(2,1)S(1)}, u32[]{:S(2)}, u32[]{:S(2)}) %collective-permute-start.4) | collective-permute-done | bytes 131104 | tf_op jit(solution)/shard_map/neighbours/ppermute | solution.py:334
  107.8 2.4 %collective-permute-done.5.rest_4_ = bf16[512,128]{1,0:T(8,128)(2,1)S(1)} collective-permute-done((bf16[512,128]{1,0:T(8,128)(2,1)S(1)}, bf16[512,128]{1,0:T(8,128)(2,1)S(1)}, u32[]{:S(2)}, u32[]{:S(2)}) %collective-permute-start.5) | collective-permute-done | bytes 131104 | tf_op jit(solution)/shard_map/neighbours/ppermute | solution.py:335
  110.3 3.0 %all-to-all-done.4 = f32[4,384,128]{2,1,0:T(8,128)S(1)} async-done(((f32[4,384,128]{2,1,0:T(8,128)}), f32[4,384,128]{2,1,0:T(8,128)S(1)}, u32[]{:S(2)}, u32[]{:S(2)}) %all-to-all-start.4) | async-done | bytes 786464 | tf_op jit(solution)/shard_map/gather_y/all_to_all | solution.py:288
  113.3 21.6 %rounds.1 = (bf16[2048,256]{1,0:T(8,128)(2,1)}, f32[1,256]{1,0:T(1,128)}) custom-call(s32[1]{0:T(128)} %bitcast.pair_ref, s32[8,13]{1,0:T(8,128)S(1)} %copy-done.4, s32[3]{0:T(128)S(1)} %bitcast.9, s32[3]{0:T(128)S(1)} %collective-permute-done.2.below_ref, s32[3]{0:T(128)S(1)} %collective-permute-done.3.above_ref, f32[1536,128]{1,0:T(8,128)S(1)} %bitcast.5, ...), custom_call_target="tpu_custom_call" | custom-call | flops 20999999488 | tf_op jit(solution)/shard_map/rounds/pallas_call | solution.py:262
Async XLA Ops:
  0.6 34.6 %collective-permute-start.1 = (bf16[2048,256]{1,0:T(8,128)(2,1)}, bf16[2048,256]{1,0:T(8,128)(2,1)S(1)}, u32[]{:S(2)}, u32[]{:S(2)}) collective-permute-start(bf16[2048,256]{1,0:T(8,128)(2,1)} %rest_7_.1), channel_id=1, source_target_pairs={{0,1},{2,0},{4,2},{6,4},{7,6},{5,7},{3,5},{1,3},{8,9},{10,8},{12,1... | collective-permute-start | bytes 3145736 | tf_op jit(solution)/shard_map/neighbours/ppermute | solution.py:295
  0.7 34.6 %collective-permute-start = (bf16[2048,256]{1,0:T(8,128)(2,1)}, bf16[2048,256]{1,0:T(8,128)(2,1)S(1)}, u32[]{:S(2)}, u32[]{:S(2)}) collective-permute-start(bf16[2048,256]{1,0:T(8,128)(2,1)} %rest_7_.1), channel_id=1, source_target_pairs={{1,0},{0,2},{2,4},{4,6},{6,7},{7,5},{5,3},{3,1},{9,8},{8,10},{10,1... | collective-permute-start | bytes 3145736 | tf_op jit(solution)/shard_map/neighbours/ppermute | solution.py:294
  2.7 1.3 copy-start
  35.2 1.1 copy-start.1
  35.2 1.3 copy-start.2
  49.2 26.7 %all-to-all-start.2 = ((f32[16,40,128]{2,1,0:T(8,128)}), f32[16,40,128]{2,1,0:T(8,128)S(1)}, u32[]{:S(2)}, u32[]{:S(2)}) async-start(f32[16,40,128]{2,1,0:T(8,128)} %get-tuple-element.29), calls=%async_computation.2 | async-start | bytes 655360 | tf_op jit(solution)/shard_map/sum_z/all_to_all | solution.py:288
  57.0 0.7 copy-start.3
  57.7 19.0 %collective-permute-start.3 = (s32[3]{0:T(128)S(1)}, s32[3]{0:T(128)S(1)}, u32[]{:S(2)}, u32[]{:S(2)}) collective-permute-start(s32[3]{0:T(128)S(1)} %bitcast.6), channel_id=1, source_target_pairs={{1,0},{2,1},{3,2},{4,3},{5,4},{6,5},{7,6},{9,8},{10,9},{11,10},{12... | collective-permute-start | bytes 44 | tf_op jit(solution)/shard_map/neighbours/ppermute | solution.py:315
  58.9 17.7 %collective-permute-start.2 = (s32[3]{0:T(128)S(1)}, s32[3]{0:T(128)S(1)}, u32[]{:S(2)}, u32[]{:S(2)}) collective-permute-start(s32[3]{0:T(128)S(1)} %bitcast.7), channel_id=1, source_target_pairs={{0,1},{1,2},{2,3},{3,4},{4,5},{5,6},{6,7},{8,9},{9,10},{10,11},{11... | collective-permute-start | bytes 44 | tf_op jit(solution)/shard_map/neighbours/ppermute | solution.py:314
  76.6 6.7 %copy-start.4 = (s32[8,13]{1,0:T(8,128)S(1)}, s32[8,13]{1,0:T(8,128)}, u32[]{:S(2)}) copy-start(s32[8,13]{1,0:T(8,128)} %constant.6.clone.table_ref) | copy-start | bytes 1252
  76.6 22.7 %all-to-all-start.3 = ((f32[16,24,128]{2,1,0:T(8,128)}), f32[16,24,128]{2,1,0:T(8,128)S(1)}, u32[]{:S(2)}, u32[]{:S(2)}) async-start(f32[16,24,128]{2,1,0:T(8,128)} %get-tuple-element.34), calls=%async_computation.3 | async-start | bytes 393216 | tf_op jit(solution)/shard_map/gather_z/all_to_all | solution.py:288
  100.3 13.0 %all-to-all-start.4 = ((f32[4,384,128]{2,1,0:T(8,128)}), f32[4,384,128]{2,1,0:T(8,128)S(1)}, u32[]{:S(2)}, u32[]{:S(2)}) async-start(f32[4,384,128]{2,1,0:T(8,128)} %broadcast_in_dim.2), calls=%async_computation.4 | async-start | bytes 1572864 | tf_op jit(solution)/shard_map/gather_y/all_to_all | solution.py:288
  103.8 4.0 %collective-permute-start.4 = (bf16[512,128]{1,0:T(8,128)(2,1)S(1)}, bf16[512,128]{1,0:T(8,128)(2,1)S(1)}, u32[]{:S(2)}, u32[]{:S(2)}) collective-permute-start(bf16[512,128]{1,0:T(8,128)(2,1)S(1)} %get-tuple-element.41.rest_3_), channel_id=1, source_target_pairs={{1,0},{0,2},{2,4},{4,6},{6,7},{7,5},{5,3},{3,1},{9,8},{8,10},{10,1... | collective-permute-start | bytes 393224 | tf_op jit(solution)/shard_map/neighbours/ppermute | solution.py:334
  105.3 5.0 %collective-permute-start.5 = (bf16[512,128]{1,0:T(8,128)(2,1)S(1)}, bf16[512,128]{1,0:T(8,128)(2,1)S(1)}, u32[]{:S(2)}, u32[]{:S(2)}) collective-permute-start(bf16[512,128]{1,0:T(8,128)(2,1)S(1)} %get-tuple-element.42.rest_2_), channel_id=1, source_target_pairs={{0,1},{2,0},{4,2},{6,4},{7,6},{5,7},{3,5},{1,3},{8,9},{10,8},{12,1... | collective-permute-start | bytes 393224 | tf_op jit(solution)/shard_map/neighbours/ppermute | solution.py:335

commit v3 on v2

--- a/solution.py
+++ b/solution.py
@@ -11,6 +11,7 @@
 POLAR_ITERS = 12
 Y_SIZE = 4
 HALF = 128
+QUARTER = 2 * HALF // Y_SIZE
 CHUNK = 256
 F32 = jnp.float32
 BF16 = jnp.bfloat16
@@ -97,12 +98,13 @@
     extra = jnp.concatenate([high[:piece], low[:piece], high[piece:], low[piece:]], axis=0).astype(BF16)
     for at in range(out_ref.shape[0]):
         out_ref[at, per_device:] = extra
-    pairs = (left_ref, own_ref), (own_ref, right_ref), (left_ref, right_ref)
-    totals = [dot(one[...], two[...], TN) for one, two in pairs]
-    for at in range(12):
-        a, b, row = at // 2 % 2, at % 2, at % 3 * HALF
-        block = totals[at // 4][a * HALF : (a + 1) * HALF, b * HALF : (b + 1) * HALF]
-        out_ref[at // 3, row : row + HALF] = block.astype(BF16)
+    pairs = (own_ref, left_ref), (own_ref, right_ref), (left_ref, right_ref)
+    for at, (one, two) in enumerate(pairs):
+        gram = dot(one[...], two[...], TN).astype(BF16)
+        for y in range(out_ref.shape[0]):
+            for half in range(2):
+                row = at * HALF + half * QUARTER
+                out_ref[y, row : row + QUARTER] = gram[y * QUARTER : (y + 1) * QUARTER, half * HALF : (half + 1) * HALF]
 
 
 def summed_y_kernel(both_ref, out_ref, diagonal_ref):
@@ -136,38 +138,44 @@
     return joined(first, apart, second)
 
 
-def block_of(part):
-    top = jnp.concatenate([part(0), part(1)], axis=1)
-    bottom = jnp.concatenate([part(2), part(3)], axis=1)
-    return jnp.concatenate([top, bottom], axis=0)
+def half_turned_kernel(cross_ref, from_left_ref, from_right_ref, out_ref):
+    for at, q_ref in enumerate((from_left_ref, from_right_ref, from_right_ref)):
+        row = at * HALF
+        gram = jnp.concatenate([cross_ref[row : row + QUARTER, :], cross_ref[row + QUARTER : row + HALF, :]], axis=1)
+        value = fine(gram, q_ref[: 2 * HALF, :], NN)
+        for y in range(out_ref.shape[0]):
+            out_ref[y, at * QUARTER : (at + 1) * QUARTER] = value
 
 
 def polar_starts(grams, signs):
     order = 2 * HALF
-    row = lax.broadcasted_iota(jnp.int32, (order, order), 0)
-    column = lax.broadcasted_iota(jnp.int32, (order, order), 1)
+    row, column = triangle((order, order))
     apart = (row < HALF) != (column < HALF)
     starts = []
     for gram, sign in zip(grams, signs):
         trace_mean = jnp.sum(jnp.where(row == column, gram, 0.0)) / order + 1e-06
         upper = jnp.where(row < column, gram, 0.0) / trace_mean
         upper = jnp.where(apart, sign * upper, upper)
-        initial = jnp.where(row == column, 1.0, 0.5 * (upper - upper.T))
-        starts.append(initial * lax.rsqrt(jnp.sum(initial * initial)))
+        starts.append(jnp.where(row == column, 1.0, 0.5 * (upper - upper.T)))
     return starts
 
 
-def refine(iterate):
+def cubed(iterate):
     high, low = split(iterate)
     square = dot(high, high, NT) + dot(high, low, NT) + dot(low, high, NT)
     sq_high, sq_low = split(square)
-    return 1.5 * iterate - 0.5 * (dot(sq_high, high, NN) + dot(sq_low, high, NN) + dot(sq_high, low, NN))
+    return dot(sq_high, high, NN) + dot(sq_low, high, NN) + dot(sq_high, low, NN)
+
+
+def first_step(start):
+    inverse = lax.rsqrt(jnp.sum(start * start))
+    return inverse * (1.5 * start - (0.5 * inverse * inverse) * cubed(start))
 
 
 def polars(grams, signs):
-    iterates = polar_starts(grams, signs)
-    for _ in range(POLAR_ITERS):
-        iterates = [refine(iterate) for iterate in iterates]
+    iterates = [first_step(start) for start in polar_starts(grams, signs)]
+    for _ in range(POLAR_ITERS - 1):
+        iterates = [1.5 * iterate - 0.5 * cubed(iterate) for iterate in iterates]
     return [iterate.astype(BF16) for iterate in iterates]
 
 
@@ -208,7 +216,7 @@
 ):
     sources, (out_ref, rms_ref), (*kept, held, arrived) = rest[:9], rest[9:11], rest[11:]
     copies = [pltpu.make_async_copy(source, place, arrived.at[at]) for at, (source, place) in enumerate(zip(sources, kept))]
-    for copy in copies:
+    for copy in copies[:6]:
         copy.start()
     gram_ref, from_left_ref, back_ref, ahead_ref, from_right_ref, mid_ref, left_ref, own_ref, right_ref = kept
     pair = pair_ref[0]
@@ -218,17 +226,21 @@
 
     for copy in copies[:6]:
         copy.wait()
-    g_lc, g_cr, g_lr = (block_of(lambda k: gram_ref[(4 * at + k) * HALF : (4 * at + k + 1) * HALF, :]) for at in range(3))
+    for copy in copies[6:]:
+        copy.start()
+    c_l, c_r, l_r = (
+        jnp.concatenate([gram_ref[y, at * QUARTER : (at + 1) * QUARTER] for y in range(Y_SIZE)], axis=0) for at in range(3)
+    )
     q_l, q_cl, q_cr, q_r = (ref[: 2 * HALF, :] for ref in (from_left_ref, back_ref, ahead_ref, from_right_ref))
     d_l, d_cl, d_cr, d_r = (
         ref[2 * HALF : 3 * HALF, :].astype(F32) + ref[3 * HALF :, :].astype(F32)
         for ref in (from_left_ref, back_ref, ahead_ref, from_right_ref)
     )
-    gram_l = joined(d_l, between(q_l, g_lc, q_cl), d_cl)
-    gram_r = joined(d_cr, between(q_cr, g_cr, q_r), d_r)
+    gram_l = joined(d_l, fine(q_cl, c_l, TN).T, d_cl)
+    gram_r = joined(d_cr, fine(q_cr, c_r, TN), d_r)
     cross = jnp.concatenate([
-        jnp.concatenate([between(q_l, g_lc, q_cr), between(q_l, g_lr, q_r)], axis=1),
-        jnp.concatenate([mid_ref[...], between(q_cl, g_cr, q_r)], axis=1),
+        jnp.concatenate([fine(q_cr, c_l, TN).T, fine(q_l, l_r, TN)], axis=1),
+        jnp.concatenate([mid_ref[...], fine(q_cl, c_r, TN)], axis=1),
     ], axis=0)
 
     e_l, e_r = polars([gram_l, gram_r], [sign_of(of_edge(edge_l), flip_l), sign_of(of_edge(edge_r), flip_r)])
@@ -287,9 +299,6 @@
     def swapped(value, count, groups):
         return lax.all_to_all(value.reshape(count, -1, HALF), "rows", 0, 0, axis_index_groups=groups, tiled=True)
 
-    def gathered(value, count, groups):
-        return swapped(jnp.broadcast_to(value[None], (count, *value.shape)), count, groups).reshape(-1, HALF)
-
     with jax.named_scope("neighbours"):
         left = lax.ppermute(snapshots, "cols", forward)
         right = lax.ppermute(snapshots, "cols", backward)
@@ -327,12 +336,15 @@
             first_round_kernel, (sent, sent, shape((HALF, HALF), F32)), "sssvv",
             (pair, table, orient, gram, diagonal), 9,
         )
-    cross, back, ahead, mid = lax.optimization_barrier((cross, back, ahead, mid))
-    with jax.named_scope("gather_y"):
-        cross = gathered(cross, Y_SIZE, along_y)
     with jax.named_scope("neighbours"):
         from_left = lax.ppermute(ahead, "cols", forward)
         from_right = lax.ppermute(back, "cols", backward)
+    cross, from_left, from_right = lax.optimization_barrier((cross, from_left, from_right))
+    with jax.named_scope("gather_y"):
+        cross = call(
+            half_turned_kernel, shape((Y_SIZE, 3 * QUARTER, HALF), F32), "vvv", (cross, from_left, from_right), 1
+        )
+        cross = swapped(cross, Y_SIZE, along_y)
     with jax.named_scope("rounds"):
         operands = (cross, from_left, back, ahead, from_right, mid, left, snapshots, right)
         rotated, column_rms = call(

time: 136 us -> 131 us (0.963)
  blocking collectives: 42.7 us -> 52.5 us
  waiting for transfers between devices: 29 us -> 19.8 us
  starting transfers between devices: 25.8 us -> 22.3 us
    all_to_all x2 -> x3, blocking collectives: 42.7 us -> 52.5 us  [swapped(): lax.all_to_all(value.reshape(count, -1, HALF), 'rows', 0, 0, axis_index_g...]
    all_to_all x3 -> x2, waiting for transfers between devices: 24 us -> 14.8 us  [swapped(): lax.all_to_all(value.reshape(count, -1, HALF), 'rows', 0, 0, axis_index_g...]
    all_to_all x3 -> x2, starting transfers between devices: 18 us -> 14.5 us  [swapped(): lax.all_to_all(value.reshape(count, -1, HALF), 'rows', 0, 0, axis_index_g...]
    pallas_call x6 -> x7, Pallas kernels: 33.5 us -> 32.9 us  [call(): pl.pallas_call(kernel, out_shape=outs, in_specs=[pl.BlockSpec(memory_spac...]
  transfers between devices with their start and end apart: 9 -> 8, of which waited for: 5 -> 4; matrix products, arithmetic and copies ran while one was open for 0% -> 0% of each run, Pallas kernels for 7% -> 8%
where the time goes in v3:
time: 131 us
  blocking collectives  52.5 us (40%)
  Pallas kernels  32.9 us (25%)
  starting transfers between devices  22.3 us (17%)
  waiting for transfers between devices  19.8 us (15%)
  local copies, waits for them, and re-layouts  2.19 us (2%)
    all_to_all x3, blocking collectives, swapped(): lax.all_to_all(value.reshape(count, -1, HALF), 'rows', 0, 0, axis_index_g...  52.5 us
    pallas_call x7, Pallas kernels, call(): pl.pallas_call(kernel, out_shape=outs, in_specs=[pl.BlockSpec(memory_spac...  32.9 us
    all_to_all x2, waiting for transfers between devices, swapped(): lax.all_to_all(value.reshape(count, -1, HALF), 'rows', 0, 0, axis_index_g...  14.8 us
    all_to_all x2, starting transfers between devices, swapped(): lax.all_to_all(value.reshape(count, -1, HALF), 'rows', 0, 0, axis_index_g...  14.5 us
    ppermute x1, starting transfers between devices, per_device(): below = lax.ppermute(orient, 'cols', [(c - 1, c) for c in range(1, pairs)])  3.03 us
  transfers between devices with their start and end apart: 8, of which 4 were waited for; matrix products, arithmetic and copies ran while one was open for 0% of the time, Pallas kernels for 8%

profile of v3, /device:TPU:32, one launch (start us, length us, event | category | flops | bytes accessed | tf_op | source)
XLA Modules:
  0.0 130.5 jit_solution(1191135345916135927)
XLA Ops:
  0.6 0.0 collective-permute-start.1
  0.7 2.0 %collective-permute-start = (bf16[2048,256]{1,0:T(8,128)(2,1)}, bf16[2048,256]{1,0:T(8,128)(2,1)S(1)}, u32[]{:S(2)}, u32[]{:S(2)}) collective-permute-start(bf16[2048,256]{1,0:T(8,128)(2,1)} %rest_7_.1), channel_id=1, source_target_pairs={{1,0},{0,2},{2,4},{4,6},{6,7},{7,5},{5,3},{3,1},{9,8},{8,10},{10,1... | collective-permute-start | bytes 3145736 | tf_op jit(solution)/shard_map/neighbours/ppermute | solution.py:303
  2.7 0.0 copy-start
  2.7 1.3 copy-done
  3.9 0.5 own_gram.1
  4.4 30.8 %all_to_all.25.gram_ref = f32[16,24,128]{2,1,0:T(8,128)S(1)} all-to-all(f32[16,24,128]{2,1,0:T(8,128)S(1)} %own_gram.1), channel_id=1, replica_groups={{0,32,64,96,128,160,192,224,256,288,320,352,384,416,448,480},{8,40,72,1..., dimensions={0} | all-to-all | bytes 393216 | tf_op jit(solution)/shard_map/own_gram/all_to_all | solution.py:300
  35.2 0.0 collective-permute-done.1.right_ref.rest_8_
  35.2 0.0 copy-start.1
  35.2 0.0 collective-permute-done.left_ref.rest_6_
  35.2 0.0 copy-start.2
  35.2 1.0 sum_y.2
  36.3 0.0 copy-done.1
  36.3 0.3 copy-done.2
  36.6 11.9 %all_to_all.26.both_ref = bf16[4,432,128]{2,1,0:T(8,128)(2,1)S(1)} all-to-all(bf16[4,432,128]{2,1,0:T(8,128)(2,1)S(1)} %sum_y.2), channel_id=1, replica_groups={{0,8,16,24},{32,40,48,56},{64,72,80,88},{96,104,112,120},{128,136,144,1..., dimensions={0} | all-to-all | bytes 884736 | tf_op jit(solution)/shard_map/sum_y/all_to_all | solution.py:300
  48.5 0.8 sum_y.3
  49.2 7.8 %all-to-all-start.2 = ((f32[16,40,128]{2,1,0:T(8,128)}), f32[16,40,128]{2,1,0:T(8,128)S(1)}, u32[]{:S(2)}, u32[]{:S(2)}) async-start(f32[16,40,128]{2,1,0:T(8,128)} %get-tuple-element.28), calls=%async_computation.2 | async-start | bytes 655360 | tf_op jit(solution)/shard_map/sum_z/all_to_all | solution.py:300
  57.0 0.0 copy-start.3
  57.0 0.6 copy-done.3
  57.7 1.3 collective-permute-start.3
  58.9 3.0 %collective-permute-start.2 = (s32[3]{0:T(128)S(1)}, s32[3]{0:T(128)S(1)}, u32[]{:S(2)}, u32[]{:S(2)}) collective-permute-start(s32[3]{0:T(128)S(1)} %bitcast.6), channel_id=1, source_target_pairs={{0,1},{1,2},{2,3},{3,4},{4,5},{5,6},{6,7},{8,9},{9,10},{10,11},{11... | collective-permute-start | bytes 44 | tf_op jit(solution)/shard_map/neighbours/ppermute | solution.py:323
  62.0 13.9 %all-to-all-done.2.both_ref = f32[16,40,128]{2,1,0:T(8,128)S(1)} async-done(((f32[16,40,128]{2,1,0:T(8,128)}), f32[16,40,128]{2,1,0:T(8,128)S(1)}, u32[]{:S(2)}, u32[]{:S(2)}) %all-to-all-start.2) | async-done | bytes 327712 | tf_op jit(solution)/shard_map/sum_z/all_to_all | solution.py:300
  75.9 0.7 sum_z.1
  76.6 0.0 collective-permute-done.3.above_ref
  76.6 0.0 collective-permute-done.2.below_ref
  76.6 0.0 copy-start.4
  76.6 6.7 %all-to-all-start.3 = ((f32[16,24,128]{2,1,0:T(8,128)}), f32[16,24,128]{2,1,0:T(8,128)S(1)}, u32[]{:S(2)}, u32[]{:S(2)}) async-start(f32[16,24,128]{2,1,0:T(8,128)} %get-tuple-element.33), calls=%async_computation.3 | async-start | bytes 393216 | tf_op jit(solution)/shard_map/gather_z/all_to_all | solution.py:300
  83.4 0.0 copy-done.4
  83.4 8.7 %first_round.1 = (bf16[512,128]{1,0:T(8,128)(2,1)S(1)}, bf16[512,128]{1,0:T(8,128)(2,1)S(1)}, f32[128,128]{1,0:T(8,128)S(1)}) custom-call(s32[1]{0:T(128)} %bitcast.pair_ref, s32[8,13]{1,0:T(8,128)S(1)} %copy-done.4, s32[3]{0:T(128)S(1)} %bitcast.7, f32[256,128]{1,0:T(8,128)S(1)} %get-tuple-element.34.gram_ref, f32[8,128]{1,0:T(8,128)S(1)} %get-tuple-element.35.diagonal_ref), custom_call_target="tpu_custom_call" | custom-call | flops 8999999488 | tf_op jit(solution)/shard_map/first_round/pallas_call | solution.py:274
  92.0 1.5 %collective-permute-start.4 = (bf16[512,128]{1,0:T(8,128)(2,1)S(1)}, bf16[512,128]{1,0:T(8,128)(2,1)S(1)}, u32[]{:S(2)}, u32[]{:S(2)}) collective-permute-start(bf16[512,128]{1,0:T(8,128)(2,1)S(1)} %get-tuple-element.36.rest_3_), channel_id=1, source_target_pairs={{1,0},{0,2},{2,4},{4,6},{6,7},{7,5},{5,3},{3,1},{9,8},{8,10},{10,1... | collective-permute-start | bytes 393224 | tf_op jit(solution)/shard_map/neighbours/ppermute | solution.py:340
  93.5 0.0 collective-permute-start.5
  93.5 2.5 %collective-permute-done.4.from_left_ref.rest_1_ = bf16[512,128]{1,0:T(8,128)(2,1)S(1)} collective-permute-done((bf16[512,128]{1,0:T(8,128)(2,1)S(1)}, bf16[512,128]{1,0:T(8,128)(2,1)S(1)}, u32[]{:S(2)}, u32[]{:S(2)}) %collective-permute-start.4) | collective-permute-done | bytes 131104 | tf_op jit(solution)/shard_map/neighbours/ppermute | solution.py:340
  96.1 2.4 %collective-permute-done.5.from_right_ref.rest_4_ = bf16[512,128]{1,0:T(8,128)(2,1)S(1)} collective-permute-done((bf16[512,128]{1,0:T(8,128)(2,1)S(1)}, bf16[512,128]{1,0:T(8,128)(2,1)S(1)}, u32[]{:S(2)}, u32[]{:S(2)}) %collective-permute-start.5) | collective-permute-done | bytes 131104 | tf_op jit(solution)/shard_map/neighbours/ppermute | solution.py:341
  98.5 0.9 all-to-all-done.3
  99.4 0.2 gather_y.1
  99.6 9.8 %all_to_all.27.rest_0_ = f32[4,192,128]{2,1,0:T(8,128)S(1)} all-to-all(f32[4,192,128]{2,1,0:T(8,128)S(1)} %gather_y.1), channel_id=1, replica_groups={{0,8,16,24},{32,40,48,56},{64,72,80,88},{96,104,112,120},{128,136,144,1..., dimensions={0} | all-to-all | bytes 786432 | tf_op jit(solution)/shard_map/gather_y/all_to_all | solution.py:300
  109.4 21.0 %rounds.1 = (bf16[2048,256]{1,0:T(8,128)(2,1)}, f32[1,256]{1,0:T(1,128)}) custom-call(s32[1]{0:T(128)} %bitcast.pair_ref, s32[8,13]{1,0:T(8,128)S(1)} %copy-done.4, s32[3]{0:T(128)S(1)} %bitcast.8, s32[3]{0:T(128)S(1)} %collective-permute-done.2.below_ref, s32[3]{0:T(128)S(1)} %collective-permute-done.3.above_ref, f32[4,192,128]{2,1,0:T(8,128)S(1)} %all_to_all.27.rest_0_, ...), custom_call_target="tpu_custom_call" | custom-call | flops 20999999488 | tf_op jit(solution)/shard_map/rounds/pallas_call | solution.py:274
Async XLA Ops:
  0.6 34.6 %collective-permute-start.1 = (bf16[2048,256]{1,0:T(8,128)(2,1)}, bf16[2048,256]{1,0:T(8,128)(2,1)S(1)}, u32[]{:S(2)}, u32[]{:S(2)}) collective-permute-start(bf16[2048,256]{1,0:T(8,128)(2,1)} %rest_7_.1), channel_id=1, source_target_pairs={{0,1},{2,0},{4,2},{6,4},{7,6},{5,7},{3,5},{1,3},{8,9},{10,8},{12,1... | collective-permute-start | bytes 3145736 | tf_op jit(solution)/shard_map/neighbours/ppermute | solution.py:304
  0.7 34.6 %collective-permute-start = (bf16[2048,256]{1,0:T(8,128)(2,1)}, bf16[2048,256]{1,0:T(8,128)(2,1)S(1)}, u32[]{:S(2)}, u32[]{:S(2)}) collective-permute-start(bf16[2048,256]{1,0:T(8,128)(2,1)} %rest_7_.1), channel_id=1, source_target_pairs={{1,0},{0,2},{2,4},{4,6},{6,7},{7,5},{5,3},{3,1},{9,8},{8,10},{10,1... | collective-permute-start | bytes 3145736 | tf_op jit(solution)/shard_map/neighbours/ppermute | solution.py:303
  2.7 1.3 copy-start
  35.2 1.1 copy-start.1
  35.2 1.3 %copy-start.2 = (bf16[2048,256]{1,0:T(8,128)(2,1)}, bf16[2048,256]{1,0:T(8,128)(2,1)S(1)}, u32[]{:S(2)}) copy-start(bf16[2048,256]{1,0:T(8,128)(2,1)S(1)} %collective-permute-done.left_ref.rest_6_) | copy-start | bytes 3145732
  49.2 26.7 %all-to-all-start.2 = ((f32[16,40,128]{2,1,0:T(8,128)}), f32[16,40,128]{2,1,0:T(8,128)S(1)}, u32[]{:S(2)}, u32[]{:S(2)}) async-start(f32[16,40,128]{2,1,0:T(8,128)} %get-tuple-element.28), calls=%async_computation.2 | async-start | bytes 655360 | tf_op jit(solution)/shard_map/sum_z/all_to_all | solution.py:300
  57.0 0.7 copy-start.3
  57.7 19.0 %collective-permute-start.3 = (s32[3]{0:T(128)S(1)}, s32[3]{0:T(128)S(1)}, u32[]{:S(2)}, u32[]{:S(2)}) collective-permute-start(s32[3]{0:T(128)S(1)} %bitcast.5), channel_id=1, source_target_pairs={{1,0},{2,1},{3,2},{4,3},{5,4},{6,5},{7,6},{9,8},{10,9},{11,10},{12... | collective-permute-start | bytes 44 | tf_op jit(solution)/shard_map/neighbours/ppermute | solution.py:324
  58.9 17.7 %collective-permute-start.2 = (s32[3]{0:T(128)S(1)}, s32[3]{0:T(128)S(1)}, u32[]{:S(2)}, u32[]{:S(2)}) collective-permute-start(s32[3]{0:T(128)S(1)} %bitcast.6), channel_id=1, source_target_pairs={{0,1},{1,2},{2,3},{3,4},{4,5},{5,6},{6,7},{8,9},{9,10},{10,11},{11... | collective-permute-start | bytes 44 | tf_op jit(solution)/shard_map/neighbours/ppermute | solution.py:323
  76.6 6.7 %copy-start.4 = (s32[8,13]{1,0:T(8,128)S(1)}, s32[8,13]{1,0:T(8,128)}, u32[]{:S(2)}) copy-start(s32[8,13]{1,0:T(8,128)} %constant.6.clone.table_ref) | copy-start | bytes 1252
  76.6 22.7 %all-to-all-start.3 = ((f32[16,24,128]{2,1,0:T(8,128)}), f32[16,24,128]{2,1,0:T(8,128)S(1)}, u32[]{:S(2)}, u32[]{:S(2)}) async-start(f32[16,24,128]{2,1,0:T(8,128)} %get-tuple-element.33), calls=%async_computation.3 | async-start | bytes 393216 | tf_op jit(solution)/shard_map/gather_z/all_to_all | solution.py:300
  92.0 4.0 %collective-permute-start.4 = (bf16[512,128]{1,0:T(8,128)(2,1)S(1)}, bf16[512,128]{1,0:T(8,128)(2,1)S(1)}, u32[]{:S(2)}, u32[]{:S(2)}) collective-permute-start(bf16[512,128]{1,0:T(8,128)(2,1)S(1)} %get-tuple-element.36.rest_3_), channel_id=1, source_target_pairs={{1,0},{0,2},{2,4},{4,6},{6,7},{7,5},{5,3},{3,1},{9,8},{8,10},{10,1... | collective-permute-start | bytes 393224 | tf_op jit(solution)/shard_map/neighbours/ppermute | solution.py:340
  93.5 5.0 %collective-permute-start.5 = (bf16[512,128]{1,0:T(8,128)(2,1)S(1)}, bf16[512,128]{1,0:T(8,128)(2,1)S(1)}, u32[]{:S(2)}, u32[]{:S(2)}) collective-permute-start(bf16[512,128]{1,0:T(8,128)(2,1)S(1)} %get-tuple-element.37.rest_2_), channel_id=1, source_target_pairs={{0,1},{2,0},{4,2},{6,4},{7,6},{5,7},{3,5},{1,3},{8,9},{10,8},{12,1... | collective-permute-start | bytes 393224 | tf_op jit(solution)/shard_map/neighbours/ppermute | solution.py:341

commit v4 on v3

--- a/solution.py
+++ b/solution.py
@@ -12,7 +12,7 @@
 Y_SIZE = 4
 HALF = 128
 QUARTER = 2 * HALF // Y_SIZE
-CHUNK = 256
+CHUNK = 512
 F32 = jnp.float32
 BF16 = jnp.bfloat16
 NT = (((1,), (1,)), ((), ()))
@@ -189,10 +189,6 @@
     return jnp.concatenate([top, bottom], axis=0)
 
 
-def between(one, gram, two):
-    return fine(one, fine(gram, two, NN), TN)
-
-
 def sign_of(flag, flip):
     return (1 - 2 * (flag ^ flip)).astype(F32)
 
@@ -201,13 +197,14 @@
     pair = pair_ref[0]
     gram = unpacked(gram_ref, diagonal_ref[:1, :])
     (turn,) = polars([gram], [sign_of(orient_ref[0], 0)])
-    q_cl, q_cr = half_of(turn, table_ref[pair, 5]), half_of(turn, table_ref[pair, 6])
-    for ref, q in ((back_ref, q_cl), (ahead_ref, q_cr)):
-        high, low = split(between(q, gram, q))
-        ref[: 2 * HALF, :] = q
+    q_c = jnp.concatenate([half_of(turn, table_ref[pair, 5]), half_of(turn, table_ref[pair, 6])], axis=1)
+    after = fine(q_c, fine(gram, q_c, NN), TN)
+    for ref, half in ((back_ref, slice(0, HALF)), (ahead_ref, slice(HALF, 2 * HALF))):
+        high, low = split(after[half, half])
+        ref[: 2 * HALF, :] = q_c[:, half]
         ref[2 * HALF : 3 * HALF, :] = high
         ref[3 * HALF :, :] = low
-    mid_ref[...] = between(q_cl, gram, q_cr)
+    mid_ref[...] = after[:HALF, HALF:]
 
 
 def rounds_kernel(
@@ -236,20 +233,24 @@
         ref[2 * HALF : 3 * HALF, :].astype(F32) + ref[3 * HALF :, :].astype(F32)
         for ref in (from_left_ref, back_ref, ahead_ref, from_right_ref)
     )
-    gram_l = joined(d_l, fine(q_cl, c_l, TN).T, d_cl)
-    gram_r = joined(d_cr, fine(q_cr, c_r, TN), d_r)
+    q_c = jnp.concatenate([q_cl, q_cr], axis=1)
+    met = fine(q_c, jnp.concatenate([c_l, c_r], axis=1), TN)
+    gram_l = joined(d_l, met[:HALF, :HALF].T, d_cl)
+    gram_r = joined(d_cr, met[HALF:, HALF:], d_r)
     cross = jnp.concatenate([
-        jnp.concatenate([fine(q_cr, c_l, TN).T, fine(q_l, l_r, TN)], axis=1),
-        jnp.concatenate([mid_ref[...], fine(q_cl, c_r, TN)], axis=1),
+        jnp.concatenate([met[HALF:, :HALF].T, fine(q_l, l_r, TN)], axis=1),
+        jnp.concatenate([mid_ref[...], met[:HALF, HALF:]], axis=1),
     ], axis=0)
 
     e_l, e_r = polars([gram_l, gram_r], [sign_of(of_edge(edge_l), flip_l), sign_of(of_edge(edge_r), flip_r)])
     v_l, v_r = half_of(e_l, take_l), half_of(e_r, take_r)
-    gram = joined(between(v_l, gram_l, v_l), between(v_l, cross, v_r), between(v_r, gram_r, v_r))
+    by_l = fine(gram_l, v_l, NN)
+    by_r = fine(jnp.concatenate([cross, gram_r], axis=0), v_r, NN)
+    top = fine(v_l, jnp.concatenate([by_l, by_r[: 2 * HALF]], axis=1), TN)
+    gram = joined(top[:, :HALF], top[:, HALF:], fine(v_r, by_r[2 * HALF :], TN))
 
     for copy in copies[6:]:
         copy.wait()
-    q_c = jnp.concatenate([q_cl, q_cr], axis=1)
     for at in range(0, held.shape[0], CHUNK):
         rows = slice(at, at + CHUNK)
         turned_l = dot(left_ref[rows, :], q_l, NN).astype(BF16)

time: 131 us -> 130 us (level)
  no operation moved by 1% of the time
where the time goes in v4:
time: 130 us
  blocking collectives  52.5 us (40%)
  Pallas kernels  31.7 us (24%)
  starting transfers between devices  22.3 us (17%)
  waiting for transfers between devices  19.9 us (15%)
  local copies, waits for them, and re-layouts  2.19 us (2%)
    all_to_all x3, blocking collectives, swapped(): lax.all_to_all(value.reshape(count, -1, HALF), 'rows', 0, 0, axis_index_g...  52.5 us
    pallas_call x7, Pallas kernels, call(): pl.pallas_call(kernel, out_shape=outs, in_specs=[pl.BlockSpec(memory_spac...  31.7 us
    all_to_all x2, waiting for transfers between devices, swapped(): lax.all_to_all(value.reshape(count, -1, HALF), 'rows', 0, 0, axis_index_g...  14.9 us
    all_to_all x2, starting transfers between devices, swapped(): lax.all_to_all(value.reshape(count, -1, HALF), 'rows', 0, 0, axis_index_g...  14.5 us
    ppermute x1, starting transfers between devices, per_device(): below = lax.ppermute(orient, 'cols', [(c - 1, c) for c in range(1, pairs)])  3.03 us
  transfers between devices with their start and end apart: 8, of which 4 were waited for; matrix products, arithmetic and copies ran while one was open for 0% of the time, Pallas kernels for 8%

profile of v4, /device:TPU:32, one launch (start us, length us, event | category | flops | bytes accessed | tf_op | source)
XLA Modules:
  0.0 129.5 jit_solution(10471692341977826082)
XLA Ops:
  0.6 0.0 collective-permute-start.1
  0.7 2.0 %collective-permute-start = (bf16[2048,256]{1,0:T(8,128)(2,1)}, bf16[2048,256]{1,0:T(8,128)(2,1)S(1)}, u32[]{:S(2)}, u32[]{:S(2)}) collective-permute-start(bf16[2048,256]{1,0:T(8,128)(2,1)} %rest_7_.1), channel_id=1, source_target_pairs={{1,0},{0,2},{2,4},{4,6},{6,7},{7,5},{5,3},{3,1},{9,8},{8,10},{10,1... | collective-permute-start | bytes 3145736 | tf_op jit(solution)/shard_map/neighbours/ppermute | solution.py:304
  2.7 0.0 copy-start
  2.7 1.3 copy-done
  3.9 0.5 own_gram.1
  4.4 30.8 %all_to_all.25.gram_ref = f32[16,24,128]{2,1,0:T(8,128)S(1)} all-to-all(f32[16,24,128]{2,1,0:T(8,128)S(1)} %own_gram.1), channel_id=1, replica_groups={{0,32,64,96,128,160,192,224,256,288,320,352,384,416,448,480},{8,40,72,1..., dimensions={0} | all-to-all | bytes 393216 | tf_op jit(solution)/shard_map/own_gram/all_to_all | solution.py:301
  35.2 0.0 collective-permute-done.1.right_ref.rest_8_
  35.2 0.0 copy-start.1
  35.2 0.0 collective-permute-done.left_ref.rest_6_
  35.2 0.0 copy-start.2
  35.2 1.0 sum_y.2
  36.3 0.0 copy-done.1
  36.3 0.3 copy-done.2
  36.6 11.9 %all_to_all.26.both_ref = bf16[4,432,128]{2,1,0:T(8,128)(2,1)S(1)} all-to-all(bf16[4,432,128]{2,1,0:T(8,128)(2,1)S(1)} %sum_y.2), channel_id=1, replica_groups={{0,8,16,24},{32,40,48,56},{64,72,80,88},{96,104,112,120},{128,136,144,1..., dimensions={0} | all-to-all | bytes 884736 | tf_op jit(solution)/shard_map/sum_y/all_to_all | solution.py:301
  48.5 0.8 sum_y.3
  49.2 7.8 %all-to-all-start.2 = ((f32[16,40,128]{2,1,0:T(8,128)}), f32[16,40,128]{2,1,0:T(8,128)S(1)}, u32[]{:S(2)}, u32[]{:S(2)}) async-start(f32[16,40,128]{2,1,0:T(8,128)} %get-tuple-element.28), calls=%async_computation.2 | async-start | bytes 655360 | tf_op jit(solution)/shard_map/sum_z/all_to_all | solution.py:301
  57.0 0.0 copy-start.3
  57.0 0.6 copy-done.3
  57.7 1.3 collective-permute-start.3
  58.9 3.0 %collective-permute-start.2 = (s32[3]{0:T(128)S(1)}, s32[3]{0:T(128)S(1)}, u32[]{:S(2)}, u32[]{:S(2)}) collective-permute-start(s32[3]{0:T(128)S(1)} %bitcast.6), channel_id=1, source_target_pairs={{0,1},{1,2},{2,3},{3,4},{4,5},{5,6},{6,7},{8,9},{9,10},{10,11},{11... | collective-permute-start | bytes 44 | tf_op jit(solution)/shard_map/neighbours/ppermute | solution.py:324
  62.0 13.9 %all-to-all-done.2.both_ref = f32[16,40,128]{2,1,0:T(8,128)S(1)} async-done(((f32[16,40,128]{2,1,0:T(8,128)}), f32[16,40,128]{2,1,0:T(8,128)S(1)}, u32[]{:S(2)}, u32[]{:S(2)}) %all-to-all-start.2) | async-done | bytes 327712 | tf_op jit(solution)/shard_map/sum_z/all_to_all | solution.py:301
  75.9 0.7 sum_z.1
  76.6 0.0 collective-permute-done.3.above_ref
  76.6 0.0 collective-permute-done.2.below_ref
  76.6 0.0 copy-start.4
  76.6 6.7 %all-to-all-start.3 = ((f32[16,24,128]{2,1,0:T(8,128)}), f32[16,24,128]{2,1,0:T(8,128)S(1)}, u32[]{:S(2)}, u32[]{:S(2)}) async-start(f32[16,24,128]{2,1,0:T(8,128)} %get-tuple-element.33), calls=%async_computation.3 | async-start | bytes 393216 | tf_op jit(solution)/shard_map/gather_z/all_to_all | solution.py:301
  83.4 0.0 copy-done.4
  83.4 8.5 %first_round.1 = (bf16[512,128]{1,0:T(8,128)(2,1)S(1)}, bf16[512,128]{1,0:T(8,128)(2,1)S(1)}, f32[128,128]{1,0:T(8,128)S(1)}) custom-call(s32[1]{0:T(128)} %bitcast.pair_ref, s32[8,13]{1,0:T(8,128)S(1)} %copy-done.4, s32[3]{0:T(128)S(1)} %bitcast.7, f32[256,128]{1,0:T(8,128)S(1)} %get-tuple-element.34.gram_ref, f32[8,128]{1,0:T(8,128)S(1)} %get-tuple-element.35.diagonal_ref), custom_call_target="tpu_custom_call" | custom-call | flops 8999999488 | tf_op jit(solution)/shard_map/first_round/pallas_call | solution.py:275
  91.9 1.5 %collective-permute-start.4 = (bf16[512,128]{1,0:T(8,128)(2,1)S(1)}, bf16[512,128]{1,0:T(8,128)(2,1)S(1)}, u32[]{:S(2)}, u32[]{:S(2)}) collective-permute-start(bf16[512,128]{1,0:T(8,128)(2,1)S(1)} %get-tuple-element.36.rest_3_), channel_id=1, source_target_pairs={{1,0},{0,2},{2,4},{4,6},{6,7},{7,5},{5,3},{3,1},{9,8},{8,10},{10,1... | collective-permute-start | bytes 393224 | tf_op jit(solution)/shard_map/neighbours/ppermute | solution.py:341
  93.4 0.0 collective-permute-start.5
  93.4 2.5 %collective-permute-done.4.from_left_ref.rest_1_ = bf16[512,128]{1,0:T(8,128)(2,1)S(1)} collective-permute-done((bf16[512,128]{1,0:T(8,128)(2,1)S(1)}, bf16[512,128]{1,0:T(8,128)(2,1)S(1)}, u32[]{:S(2)}, u32[]{:S(2)}) %collective-permute-start.4) | collective-permute-done | bytes 131104 | tf_op jit(solution)/shard_map/neighbours/ppermute | solution.py:341
  95.9 2.4 %collective-permute-done.5.from_right_ref.rest_4_ = bf16[512,128]{1,0:T(8,128)(2,1)S(1)} collective-permute-done((bf16[512,128]{1,0:T(8,128)(2,1)S(1)}, bf16[512,128]{1,0:T(8,128)(2,1)S(1)}, u32[]{:S(2)}, u32[]{:S(2)}) %collective-permute-start.5) | collective-permute-done | bytes 131104 | tf_op jit(solution)/shard_map/neighbours/ppermute | solution.py:342
  98.4 1.0 all-to-all-done.3
  99.4 0.2 gather_y.1
  99.6 9.8 %all_to_all.27.rest_0_ = f32[4,192,128]{2,1,0:T(8,128)S(1)} all-to-all(f32[4,192,128]{2,1,0:T(8,128)S(1)} %gather_y.1), channel_id=1, replica_groups={{0,8,16,24},{32,40,48,56},{64,72,80,88},{96,104,112,120},{128,136,144,1..., dimensions={0} | all-to-all | bytes 786432 | tf_op jit(solution)/shard_map/gather_y/all_to_all | solution.py:301
  109.4 20.0 %rounds.1 = (bf16[2048,256]{1,0:T(8,128)(2,1)}, f32[1,256]{1,0:T(1,128)}) custom-call(s32[1]{0:T(128)} %bitcast.pair_ref, s32[8,13]{1,0:T(8,128)S(1)} %copy-done.4, s32[3]{0:T(128)S(1)} %bitcast.8, s32[3]{0:T(128)S(1)} %collective-permute-done.2.below_ref, s32[3]{0:T(128)S(1)} %collective-permute-done.3.above_ref, f32[4,192,128]{2,1,0:T(8,128)S(1)} %all_to_all.27.rest_0_, ...), custom_call_target="tpu_custom_call" | custom-call | flops 20999999488 | tf_op jit(solution)/shard_map/rounds/pallas_call | solution.py:275
Async XLA Ops:
  0.6 34.6 %collective-permute-start.1 = (bf16[2048,256]{1,0:T(8,128)(2,1)}, bf16[2048,256]{1,0:T(8,128)(2,1)S(1)}, u32[]{:S(2)}, u32[]{:S(2)}) collective-permute-start(bf16[2048,256]{1,0:T(8,128)(2,1)} %rest_7_.1), channel_id=1, source_target_pairs={{0,1},{2,0},{4,2},{6,4},{7,6},{5,7},{3,5},{1,3},{8,9},{10,8},{12,1... | collective-permute-start | bytes 3145736 | tf_op jit(solution)/shard_map/neighbours/ppermute | solution.py:305
  0.7 34.6 %collective-permute-start = (bf16[2048,256]{1,0:T(8,128)(2,1)}, bf16[2048,256]{1,0:T(8,128)(2,1)S(1)}, u32[]{:S(2)}, u32[]{:S(2)}) collective-permute-start(bf16[2048,256]{1,0:T(8,128)(2,1)} %rest_7_.1), channel_id=1, source_target_pairs={{1,0},{0,2},{2,4},{4,6},{6,7},{7,5},{5,3},{3,1},{9,8},{8,10},{10,1... | collective-permute-start | bytes 3145736 | tf_op jit(solution)/shard_map/neighbours/ppermute | solution.py:304
  2.7 1.3 copy-start
  35.2 1.1 copy-start.1
  35.2 1.3 %copy-start.2 = (bf16[2048,256]{1,0:T(8,128)(2,1)}, bf16[2048,256]{1,0:T(8,128)(2,1)S(1)}, u32[]{:S(2)}) copy-start(bf16[2048,256]{1,0:T(8,128)(2,1)S(1)} %collective-permute-done.left_ref.rest_6_) | copy-start | bytes 3145732
  49.2 26.7 %all-to-all-start.2 = ((f32[16,40,128]{2,1,0:T(8,128)}), f32[16,40,128]{2,1,0:T(8,128)S(1)}, u32[]{:S(2)}, u32[]{:S(2)}) async-start(f32[16,40,128]{2,1,0:T(8,128)} %get-tuple-element.28), calls=%async_computation.2 | async-start | bytes 655360 | tf_op jit(solution)/shard_map/sum_z/all_to_all | solution.py:301
  57.0 0.7 copy-start.3
  57.7 19.0 %collective-permute-start.3 = (s32[3]{0:T(128)S(1)}, s32[3]{0:T(128)S(1)}, u32[]{:S(2)}, u32[]{:S(2)}) collective-permute-start(s32[3]{0:T(128)S(1)} %bitcast.5), channel_id=1, source_target_pairs={{1,0},{2,1},{3,2},{4,3},{5,4},{6,5},{7,6},{9,8},{10,9},{11,10},{12... | collective-permute-start | bytes 44 | tf_op jit(solution)/shard_map/neighbours/ppermute | solution.py:325
  58.9 17.7 %collective-permute-start.2 = (s32[3]{0:T(128)S(1)}, s32[3]{0:T(128)S(1)}, u32[]{:S(2)}, u32[]{:S(2)}) collective-permute-start(s32[3]{0:T(128)S(1)} %bitcast.6), channel_id=1, source_target_pairs={{0,1},{1,2},{2,3},{3,4},{4,5},{5,6},{6,7},{8,9},{9,10},{10,11},{11... | collective-permute-start | bytes 44 | tf_op jit(solution)/shard_map/neighbours/ppermute | solution.py:324
  76.6 6.7 %copy-start.4 = (s32[8,13]{1,0:T(8,128)S(1)}, s32[8,13]{1,0:T(8,128)}, u32[]{:S(2)}) copy-start(s32[8,13]{1,0:T(8,128)} %constant.6.clone.table_ref) | copy-start | bytes 1252
  76.6 22.7 %all-to-all-start.3 = ((f32[16,24,128]{2,1,0:T(8,128)}), f32[16,24,128]{2,1,0:T(8,128)S(1)}, u32[]{:S(2)}, u32[]{:S(2)}) async-start(f32[16,24,128]{2,1,0:T(8,128)} %get-tuple-element.33), calls=%async_computation.3 | async-start | bytes 393216 | tf_op jit(solution)/shard_map/gather_z/all_to_all | solution.py:301
  91.9 4.0 %collective-permute-start.4 = (bf16[512,128]{1,0:T(8,128)(2,1)S(1)}, bf16[512,128]{1,0:T(8,128)(2,1)S(1)}, u32[]{:S(2)}, u32[]{:S(2)}) collective-permute-start(bf16[512,128]{1,0:T(8,128)(2,1)S(1)} %get-tuple-element.36.rest_3_), channel_id=1, source_target_pairs={{1,0},{0,2},{2,4},{4,6},{6,7},{7,5},{5,3},{3,1},{9,8},{8,10},{10,1... | collective-permute-start | bytes 393224 | tf_op jit(solution)/shard_map/neighbours/ppermute | solution.py:341
  93.4 5.0 %collective-permute-start.5 = (bf16[512,128]{1,0:T(8,128)(2,1)S(1)}, bf16[512,128]{1,0:T(8,128)(2,1)S(1)}, u32[]{:S(2)}, u32[]{:S(2)}) collective-permute-start(bf16[512,128]{1,0:T(8,128)(2,1)S(1)} %get-tuple-element.37.rest_2_), channel_id=1, source_target_pairs={{0,1},{2,0},{4,2},{6,4},{7,6},{5,7},{3,5},{1,3},{8,9},{10,8},{12,1... | collective-permute-start | bytes 393224 | tf_op jit(solution)/shard_map/neighbours/ppermute | solution.py:342

commit v5 on v4

--- a/solution.py
+++ b/solution.py
@@ -84,15 +84,15 @@
     row, column = triangle(first.shape)
     diagonal = jnp.sum(jnp.where(row == column, second, 0.0), axis=0, keepdims=True)
     packed = jnp.concatenate([jnp.where(row <= column, first, second), apart], axis=0)
-    pieces, rows = out_ref.shape[0], out_ref.shape[1] - 8
+    pieces, rows = out_ref.shape[0], out_ref.shape[1] - 16
     for at in range(pieces):
-        out_ref[at, :rows] = packed[at * rows : (at + 1) * rows]
-        out_ref[at, rows:] = jnp.broadcast_to(diagonal, (8, HALF))
+        out_ref[at, :rows] = packed[at * rows : (at + 1) * rows].astype(BF16)
+        out_ref[at, rows:] = jnp.broadcast_to(diagonal, (16, HALF)).astype(BF16)
 
 
 def cross_gram_kernel(left_ref, own_ref, right_ref, gram_ref, out_ref):
-    per_device, piece = 3 * HALF, gram_ref.shape[1] - 8
-    total = jnp.sum(gram_ref[...], axis=0)
+    per_device, piece = 3 * HALF, gram_ref.shape[1] - 16
+    total = jnp.sum(gram_ref[...].astype(F32), axis=0)[: piece + 8]
     high = total.astype(BF16).astype(F32)
     low = total - high
     extra = jnp.concatenate([high[:piece], low[:piece], high[piece:], low[piece:]], axis=0).astype(BF16)
@@ -306,7 +306,7 @@
     with jax.named_scope("own_gram"):
         piece, step = 2 * HALF // z_size, 3 * HALF // z_size
         gram = call(
-            own_gram_kernel, shape((z_size, piece + 8, HALF), F32), "v", (snapshots,), 1
+            own_gram_kernel, shape((z_size, piece + 16, HALF), BF16), "v", (snapshots,), 1
         )
         gram = swapped(gram, z_size, along_z)
     left, right, gram = lax.optimization_barrier((left, right, gram))

time: 130 us -> 130 us (level)
  starting transfers between devices: 22.3 us -> 25.1 us
  blocking collectives: 52.5 us -> 49.7 us
    all_to_all x3, blocking collectives: 52.5 us -> 49.7 us  [swapped(): lax.all_to_all(value.reshape(count, -1, HALF), 'rows', 0, 0, axis_index_g...]
    all_to_all x2, starting transfers between devices: 14.5 us -> 17.2 us  [swapped(): lax.all_to_all(value.reshape(count, -1, HALF), 'rows', 0, 0, axis_index_g...]
where the time goes in v5:
time: 130 us
  blocking collectives  49.7 us (38%)
  Pallas kernels  31.7 us (24%)
  starting transfers between devices  25.1 us (19%)
  waiting for transfers between devices  19.9 us (15%)
  local copies, waits for them, and re-layouts  2.19 us (2%)
    all_to_all x3, blocking collectives, swapped(): lax.all_to_all(value.reshape(count, -1, HALF), 'rows', 0, 0, axis_index_g...  49.7 us
    pallas_call x7, Pallas kernels, call(): pl.pallas_call(kernel, out_shape=outs, in_specs=[pl.BlockSpec(memory_spac...  31.7 us
    all_to_all x2, starting transfers between devices, swapped(): lax.all_to_all(value.reshape(count, -1, HALF), 'rows', 0, 0, axis_index_g...  17.2 us
    all_to_all x2, waiting for transfers between devices, swapped(): lax.all_to_all(value.reshape(count, -1, HALF), 'rows', 0, 0, axis_index_g...  14.9 us
    ppermute x1, starting transfers between devices, per_device(): below = lax.ppermute(orient, 'cols', [(c - 1, c) for c in range(1, pairs)])  3.03 us
  transfers between devices with their start and end apart: 8, of which 4 were waited for; matrix products, arithmetic and copies ran while one was open for 0% of the time, Pallas kernels for 8%

profile of v5, /device:TPU:32, one launch (start us, length us, event | category | flops | bytes accessed | tf_op | source)
XLA Modules:
  0.0 129.5 jit_solution(12324604065037048112)
XLA Ops:
  0.6 0.0 collective-permute-start.1
  0.7 2.0 %collective-permute-start = (bf16[2048,256]{1,0:T(8,128)(2,1)}, bf16[2048,256]{1,0:T(8,128)(2,1)S(1)}, u32[]{:S(2)}, u32[]{:S(2)}) collective-permute-start(bf16[2048,256]{1,0:T(8,128)(2,1)} %rest_7_.1), channel_id=1, source_target_pairs={{1,0},{0,2},{2,4},{4,6},{6,7},{7,5},{5,3},{3,1},{9,8},{8,10},{10,1... | collective-permute-start | bytes 3145736 | tf_op jit(solution)/shard_map/neighbours/ppermute | solution.py:304
  2.7 0.0 copy-start
  2.7 1.3 copy-done
  3.9 0.5 own_gram.1
  4.4 28.1 %all_to_all.25.gram_ref = bf16[16,32,128]{2,1,0:T(8,128)(2,1)S(1)} all-to-all(bf16[16,32,128]{2,1,0:T(8,128)(2,1)S(1)} %own_gram.1), channel_id=1, replica_groups={{0,32,64,96,128,160,192,224,256,288,320,352,384,416,448,480},{8,40,72,1..., dimensions={0} | all-to-all | bytes 262144 | tf_op jit(solution)/shard_map/own_gram/all_to_all | solution.py:301
  32.5 0.0 collective-permute-done.1.right_ref.rest_8_
  32.5 0.0 copy-start.1
  32.5 0.0 collective-permute-done.left_ref.rest_6_
  32.5 0.0 copy-start.2
  32.5 1.0 sum_y.2
  33.5 0.0 copy-done.1
  33.6 0.3 copy-done.2
  33.8 11.9 %all_to_all.26.both_ref = bf16[4,432,128]{2,1,0:T(8,128)(2,1)S(1)} all-to-all(bf16[4,432,128]{2,1,0:T(8,128)(2,1)S(1)} %sum_y.2), channel_id=1, replica_groups={{0,8,16,24},{32,40,48,56},{64,72,80,88},{96,104,112,120},{128,136,144,1..., dimensions={0} | all-to-all | bytes 884736 | tf_op jit(solution)/shard_map/sum_y/all_to_all | solution.py:301
  45.7 0.8 sum_y.3
  46.5 10.5 %all-to-all-start.2 = ((f32[16,40,128]{2,1,0:T(8,128)}), f32[16,40,128]{2,1,0:T(8,128)S(1)}, u32[]{:S(2)}, u32[]{:S(2)}) async-start(f32[16,40,128]{2,1,0:T(8,128)} %get-tuple-element.28), calls=%async_computation.2 | async-start | bytes 655360 | tf_op jit(solution)/shard_map/sum_z/all_to_all | solution.py:301
  57.0 0.0 copy-start.3
  57.0 0.6 copy-done.3
  57.7 1.3 collective-permute-start.3
  58.9 3.0 %collective-permute-start.2 = (s32[3]{0:T(128)S(1)}, s32[3]{0:T(128)S(1)}, u32[]{:S(2)}, u32[]{:S(2)}) collective-permute-start(s32[3]{0:T(128)S(1)} %bitcast.6), channel_id=1, source_target_pairs={{0,1},{1,2},{2,3},{3,4},{4,5},{5,6},{6,7},{8,9},{9,10},{10,11},{11... | collective-permute-start | bytes 44 | tf_op jit(solution)/shard_map/neighbours/ppermute | solution.py:324
  62.0 13.9 %all-to-all-done.2.both_ref = f32[16,40,128]{2,1,0:T(8,128)S(1)} async-done(((f32[16,40,128]{2,1,0:T(8,128)}), f32[16,40,128]{2,1,0:T(8,128)S(1)}, u32[]{:S(2)}, u32[]{:S(2)}) %all-to-all-start.2) | async-done | bytes 327712 | tf_op jit(solution)/shard_map/sum_z/all_to_all | solution.py:301
  75.9 0.7 sum_z.1
  76.6 0.0 collective-permute-done.3.above_ref
  76.6 0.0 collective-permute-done.2.below_ref
  76.6 0.0 copy-start.4
  76.6 6.7 %all-to-all-start.3 = ((f32[16,24,128]{2,1,0:T(8,128)}), f32[16,24,128]{2,1,0:T(8,128)S(1)}, u32[]{:S(2)}, u32[]{:S(2)}) async-start(f32[16,24,128]{2,1,0:T(8,128)} %get-tuple-element.33), calls=%async_computation.3 | async-start | bytes 393216 | tf_op jit(solution)/shard_map/gather_z/all_to_all | solution.py:301
  83.4 0.0 copy-done.4
  83.4 8.5 %first_round.1 = (bf16[512,128]{1,0:T(8,128)(2,1)S(1)}, bf16[512,128]{1,0:T(8,128)(2,1)S(1)}, f32[128,128]{1,0:T(8,128)S(1)}) custom-call(s32[1]{0:T(128)} %bitcast.pair_ref, s32[8,13]{1,0:T(8,128)S(1)} %copy-done.4, s32[3]{0:T(128)S(1)} %bitcast.7, f32[256,128]{1,0:T(8,128)S(1)} %get-tuple-element.34.gram_ref, f32[8,128]{1,0:T(8,128)S(1)} %get-tuple-element.35.diagonal_ref), custom_call_target="tpu_custom_call" | custom-call | flops 8999999488 | tf_op jit(solution)/shard_map/first_round/pallas_call | solution.py:275
  91.9 1.5 %collective-permute-start.4 = (bf16[512,128]{1,0:T(8,128)(2,1)S(1)}, bf16[512,128]{1,0:T(8,128)(2,1)S(1)}, u32[]{:S(2)}, u32[]{:S(2)}) collective-permute-start(bf16[512,128]{1,0:T(8,128)(2,1)S(1)} %get-tuple-element.36.rest_3_), channel_id=1, source_target_pairs={{1,0},{0,2},{2,4},{4,6},{6,7},{7,5},{5,3},{3,1},{9,8},{8,10},{10,1... | collective-permute-start | bytes 393224 | tf_op jit(solution)/shard_map/neighbours/ppermute | solution.py:341
  93.4 0.0 collective-permute-start.5
  93.4 2.5 %collective-permute-done.4.from_left_ref.rest_1_ = bf16[512,128]{1,0:T(8,128)(2,1)S(1)} collective-permute-done((bf16[512,128]{1,0:T(8,128)(2,1)S(1)}, bf16[512,128]{1,0:T(8,128)(2,1)S(1)}, u32[]{:S(2)}, u32[]{:S(2)}) %collective-permute-start.4) | collective-permute-done | bytes 131104 | tf_op jit(solution)/shard_map/neighbours/ppermute | solution.py:341
  95.9 2.4 %collective-permute-done.5.from_right_ref.rest_4_ = bf16[512,128]{1,0:T(8,128)(2,1)S(1)} collective-permute-done((bf16[512,128]{1,0:T(8,128)(2,1)S(1)}, bf16[512,128]{1,0:T(8,128)(2,1)S(1)}, u32[]{:S(2)}, u32[]{:S(2)}) %collective-permute-start.5) | collective-permute-done | bytes 131104 | tf_op jit(solution)/shard_map/neighbours/ppermute | solution.py:342
  98.4 1.0 all-to-all-done.3
  99.4 0.2 gather_y.1
  99.6 9.8 %all_to_all.27.rest_0_ = f32[4,192,128]{2,1,0:T(8,128)S(1)} all-to-all(f32[4,192,128]{2,1,0:T(8,128)S(1)} %gather_y.1), channel_id=1, replica_groups={{0,8,16,24},{32,40,48,56},{64,72,80,88},{96,104,112,120},{128,136,144,1..., dimensions={0} | all-to-all | bytes 786432 | tf_op jit(solution)/shard_map/gather_y/all_to_all | solution.py:301
  109.4 20.0 %rounds.1 = (bf16[2048,256]{1,0:T(8,128)(2,1)}, f32[1,256]{1,0:T(1,128)}) custom-call(s32[1]{0:T(128)} %bitcast.pair_ref, s32[8,13]{1,0:T(8,128)S(1)} %copy-done.4, s32[3]{0:T(128)S(1)} %bitcast.8, s32[3]{0:T(128)S(1)} %collective-permute-done.2.below_ref, s32[3]{0:T(128)S(1)} %collective-permute-done.3.above_ref, f32[4,192,128]{2,1,0:T(8,128)S(1)} %all_to_all.27.rest_0_, ...), custom_call_target="tpu_custom_call" | custom-call | flops 20999999488 | tf_op jit(solution)/shard_map/rounds/pallas_call | solution.py:275
Async XLA Ops:
  0.6 31.9 %collective-permute-start.1 = (bf16[2048,256]{1,0:T(8,128)(2,1)}, bf16[2048,256]{1,0:T(8,128)(2,1)S(1)}, u32[]{:S(2)}, u32[]{:S(2)}) collective-permute-start(bf16[2048,256]{1,0:T(8,128)(2,1)} %rest_7_.1), channel_id=1, source_target_pairs={{0,1},{2,0},{4,2},{6,4},{7,6},{5,7},{3,5},{1,3},{8,9},{10,8},{12,1... | collective-permute-start | bytes 3145736 | tf_op jit(solution)/shard_map/neighbours/ppermute | solution.py:305
  0.7 31.8 %collective-permute-start = (bf16[2048,256]{1,0:T(8,128)(2,1)}, bf16[2048,256]{1,0:T(8,128)(2,1)S(1)}, u32[]{:S(2)}, u32[]{:S(2)}) collective-permute-start(bf16[2048,256]{1,0:T(8,128)(2,1)} %rest_7_.1), channel_id=1, source_target_pairs={{1,0},{0,2},{2,4},{4,6},{6,7},{7,5},{5,3},{3,1},{9,8},{8,10},{10,1... | collective-permute-start | bytes 3145736 | tf_op jit(solution)/shard_map/neighbours/ppermute | solution.py:304
  2.7 1.3 copy-start
  32.5 1.1 copy-start.1
  32.5 1.3 %copy-start.2 = (bf16[2048,256]{1,0:T(8,128)(2,1)}, bf16[2048,256]{1,0:T(8,128)(2,1)S(1)}, u32[]{:S(2)}) copy-start(bf16[2048,256]{1,0:T(8,128)(2,1)S(1)} %collective-permute-done.left_ref.rest_6_) | copy-start | bytes 3145732
  46.5 29.4 %all-to-all-start.2 = ((f32[16,40,128]{2,1,0:T(8,128)}), f32[16,40,128]{2,1,0:T(8,128)S(1)}, u32[]{:S(2)}, u32[]{:S(2)}) async-start(f32[16,40,128]{2,1,0:T(8,128)} %get-tuple-element.28), calls=%async_computation.2 | async-start | bytes 655360 | tf_op jit(solution)/shard_map/sum_z/all_to_all | solution.py:301
  57.0 0.7 copy-start.3
  57.7 19.0 %collective-permute-start.3 = (s32[3]{0:T(128)S(1)}, s32[3]{0:T(128)S(1)}, u32[]{:S(2)}, u32[]{:S(2)}) collective-permute-start(s32[3]{0:T(128)S(1)} %bitcast.5), channel_id=1, source_target_pairs={{1,0},{2,1},{3,2},{4,3},{5,4},{6,5},{7,6},{9,8},{10,9},{11,10},{12... | collective-permute-start | bytes 44 | tf_op jit(solution)/shard_map/neighbours/ppermute | solution.py:325
  58.9 17.7 %collective-permute-start.2 = (s32[3]{0:T(128)S(1)}, s32[3]{0:T(128)S(1)}, u32[]{:S(2)}, u32[]{:S(2)}) collective-permute-start(s32[3]{0:T(128)S(1)} %bitcast.6), channel_id=1, source_target_pairs={{0,1},{1,2},{2,3},{3,4},{4,5},{5,6},{6,7},{8,9},{9,10},{10,11},{11... | collective-permute-start | bytes 44 | tf_op jit(solution)/shard_map/neighbours/ppermute | solution.py:324
  76.6 6.7 %copy-start.4 = (s32[8,13]{1,0:T(8,128)S(1)}, s32[8,13]{1,0:T(8,128)}, u32[]{:S(2)}) copy-start(s32[8,13]{1,0:T(8,128)} %constant.6.clone.table_ref) | copy-start | bytes 1252
  76.6 22.7 %all-to-all-start.3 = ((f32[16,24,128]{2,1,0:T(8,128)}), f32[16,24,128]{2,1,0:T(8,128)S(1)}, u32[]{:S(2)}, u32[]{:S(2)}) async-start(f32[16,24,128]{2,1,0:T(8,128)} %get-tuple-element.33), calls=%async_computation.3 | async-start | bytes 393216 | tf_op jit(solution)/shard_map/gather_z/all_to_all | solution.py:301
  91.9 4.0 %collective-permute-start.4 = (bf16[512,128]{1,0:T(8,128)(2,1)S(1)}, bf16[512,128]{1,0:T(8,128)(2,1)S(1)}, u32[]{:S(2)}, u32[]{:S(2)}) collective-permute-start(bf16[512,128]{1,0:T(8,128)(2,1)S(1)} %get-tuple-element.36.rest_3_), channel_id=1, source_target_pairs={{1,0},{0,2},{2,4},{4,6},{6,7},{7,5},{5,3},{3,1},{9,8},{8,10},{10,1... | collective-permute-start | bytes 393224 | tf_op jit(solution)/shard_map/neighbours/ppermute | solution.py:341
  93.4 5.0 %collective-permute-start.5 = (bf16[512,128]{1,0:T(8,128)(2,1)S(1)}, bf16[512,128]{1,0:T(8,128)(2,1)S(1)}, u32[]{:S(2)}, u32[]{:S(2)}) collective-permute-start(bf16[512,128]{1,0:T(8,128)(2,1)S(1)} %get-tuple-element.37.rest_2_), channel_id=1, source_target_pairs={{0,1},{2,0},{4,2},{6,4},{7,6},{5,7},{3,5},{1,3},{8,9},{10,8},{12,1... | collective-permute-start | bytes 393224 | tf_op jit(solution)/shard_map/neighbours/ppermute | solution.py:342

commit v6 on v4

--- a/solution.py
+++ b/solution.py
@@ -211,20 +211,17 @@
     total_rows, pair_ref, table_ref, orient_ref, below_ref, above_ref,
     *rest,
 ):
-    sources, (out_ref, rms_ref), (*kept, held, arrived) = rest[:9], rest[9:11], rest[11:]
+    gram_ref, from_left_ref, back_ref, ahead_ref, from_right_ref, mid_ref = rest[:6]
+    sources, (out_ref, rms_ref), (*kept, held, arrived) = rest[6:9], rest[9:11], rest[11:]
     copies = [pltpu.make_async_copy(source, place, arrived.at[at]) for at, (source, place) in enumerate(zip(sources, kept))]
-    for copy in copies[:6]:
+    for copy in copies:
         copy.start()
-    gram_ref, from_left_ref, back_ref, ahead_ref, from_right_ref, mid_ref, left_ref, own_ref, right_ref = kept
+    left_ref, own_ref, right_ref = kept
     pair = pair_ref[0]
     look = lambda at: table_ref[pair, at]
     edge_l, edge_r, flip_l, flip_r, take_l, take_r, swap = (look(at) for at in (2, 3, 8, 9, 10, 11, 12))
     of_edge = lambda edge: jnp.where(edge < pair, below_ref[1], jnp.where(edge > pair, above_ref[1], orient_ref[1]))
 
-    for copy in copies[:6]:
-        copy.wait()
-    for copy in copies[6:]:
-        copy.start()
     c_l, c_r, l_r = (
         jnp.concatenate([gram_ref[y, at * QUARTER : (at + 1) * QUARTER] for y in range(Y_SIZE)], axis=0) for at in range(3)
     )
@@ -249,7 +246,7 @@
     top = fine(v_l, jnp.concatenate([by_l, by_r[: 2 * HALF]], axis=1), TN)
     gram = joined(top[:, :HALF], top[:, HALF:], fine(v_r, by_r[2 * HALF :], TN))
 
-    for copy in copies[6:]:
+    for copy in copies:
         copy.wait()
     for at in range(0, held.shape[0], CHUNK):
         rows = slice(at, at + CHUNK)
@@ -347,15 +344,16 @@
         )
         cross = swapped(cross, Y_SIZE, along_y)
     with jax.named_scope("rounds"):
-        operands = (cross, from_left, back, ahead, from_right, mid, left, snapshots, right)
+        operands = (cross, from_left, back, ahead, from_right, mid)
+        columns = (left, snapshots, right)
         rotated, column_rms = call(
             functools.partial(rounds_kernel, height * rows_axis),
             (shape(snapshots.shape, BF16), shape((1, 2 * HALF), F32)),
-            "sssss" + "a" * len(operands),
-            (pair, table, orient, below, above, *operands),
+            "sssss" + "v" * len(operands) + "a" * len(columns),
+            (pair, table, orient, below, above, *operands, *columns),
             21,
-            [pltpu.VMEM(value.shape, value.dtype) for value in operands]
-            + [pltpu.VMEM(snapshots.shape, BF16), pltpu.SemaphoreType.DMA((len(operands),))],
+            [pltpu.VMEM(value.shape, value.dtype) for value in columns]
+            + [pltpu.VMEM(snapshots.shape, BF16), pltpu.SemaphoreType.DMA((len(columns),))],
             megabytes=52,
         )
     return rotated, column_rms.reshape(-1)

time: 130 us -> 130 us (level)
  transfers between devices with their start and end apart: 8 -> 8, of which waited for: 4 -> 4; matrix products, arithmetic and copies ran while one was open for 0% -> 0% of each run, Pallas kernels for 8% -> 7%
where the time goes in v6:
time: 130 us
  blocking collectives  52.5 us (40%)
  Pallas kernels  32 us (25%)
  starting transfers between devices  22.3 us (17%)
  waiting for transfers between devices  19.9 us (15%)
  local copies, waits for them, and re-layouts  2.19 us (2%)
    all_to_all x3, blocking collectives, swapped(): lax.all_to_all(value.reshape(count, -1, HALF), 'rows', 0, 0, axis_index_g...  52.5 us
    pallas_call x7, Pallas kernels, call(): pl.pallas_call(kernel, out_shape=outs, in_specs=[pl.BlockSpec(memory_spac...  32 us
    all_to_all x2, waiting for transfers between devices, swapped(): lax.all_to_all(value.reshape(count, -1, HALF), 'rows', 0, 0, axis_index_g...  14.9 us
    all_to_all x2, starting transfers between devices, swapped(): lax.all_to_all(value.reshape(count, -1, HALF), 'rows', 0, 0, axis_index_g...  14.5 us
    ppermute x1, starting transfers between devices, per_device(): below = lax.ppermute(orient, 'cols', [(c - 1, c) for c in range(1, pairs)])  3.03 us
  transfers between devices with their start and end apart: 8, of which 4 were waited for; matrix products, arithmetic and copies ran while one was open for 0% of the time, Pallas kernels for 7%

profile of v6, /device:TPU:32, one launch (start us, length us, event | category | flops | bytes accessed | tf_op | source)
XLA Modules:
  0.0 129.8 jit_solution(1736105526009986101)
XLA Ops:
  0.6 0.0 collective-permute-start.1
  0.7 2.0 %collective-permute-start = (bf16[2048,256]{1,0:T(8,128)(2,1)}, bf16[2048,256]{1,0:T(8,128)(2,1)S(1)}, u32[]{:S(2)}, u32[]{:S(2)}) collective-permute-start(bf16[2048,256]{1,0:T(8,128)(2,1)} %rest_7_.1), channel_id=1, source_target_pairs={{1,0},{0,2},{2,4},{4,6},{6,7},{7,5},{5,3},{3,1},{9,8},{8,10},{10,1... | collective-permute-start | bytes 3145736 | tf_op jit(solution)/shard_map/neighbours/ppermute | solution.py:301
  2.7 0.0 copy-start
  2.7 1.3 copy-done
  3.9 0.5 own_gram.1
  4.4 30.8 %all_to_all.25.gram_ref = f32[16,24,128]{2,1,0:T(8,128)S(1)} all-to-all(f32[16,24,128]{2,1,0:T(8,128)S(1)} %own_gram.1), channel_id=1, replica_groups={{0,32,64,96,128,160,192,224,256,288,320,352,384,416,448,480},{8,40,72,1..., dimensions={0} | all-to-all | bytes 393216 | tf_op jit(solution)/shard_map/own_gram/all_to_all | solution.py:298
  35.2 0.0 collective-permute-done.1.right_ref.rest_8_
  35.2 0.0 copy-start.1
  35.2 0.0 collective-permute-done.left_ref.rest_6_
  35.2 0.0 copy-start.2
  35.2 1.0 sum_y.2
  36.3 0.0 copy-done.1
  36.3 0.3 copy-done.2
  36.6 11.9 %all_to_all.26.both_ref = bf16[4,432,128]{2,1,0:T(8,128)(2,1)S(1)} all-to-all(bf16[4,432,128]{2,1,0:T(8,128)(2,1)S(1)} %sum_y.2), channel_id=1, replica_groups={{0,8,16,24},{32,40,48,56},{64,72,80,88},{96,104,112,120},{128,136,144,1..., dimensions={0} | all-to-all | bytes 884736 | tf_op jit(solution)/shard_map/sum_y/all_to_all | solution.py:298
  48.5 0.8 sum_y.3
  49.2 7.8 %all-to-all-start.2 = ((f32[16,40,128]{2,1,0:T(8,128)}), f32[16,40,128]{2,1,0:T(8,128)S(1)}, u32[]{:S(2)}, u32[]{:S(2)}) async-start(f32[16,40,128]{2,1,0:T(8,128)} %get-tuple-element.28), calls=%async_computation.2 | async-start | bytes 655360 | tf_op jit(solution)/shard_map/sum_z/all_to_all | solution.py:298
  57.0 0.0 copy-start.3
  57.0 0.6 copy-done.3
  57.7 1.3 collective-permute-start.3
  58.9 3.0 %collective-permute-start.2 = (s32[3]{0:T(128)S(1)}, s32[3]{0:T(128)S(1)}, u32[]{:S(2)}, u32[]{:S(2)}) collective-permute-start(s32[3]{0:T(128)S(1)} %bitcast.6), channel_id=1, source_target_pairs={{0,1},{1,2},{2,3},{3,4},{4,5},{5,6},{6,7},{8,9},{9,10},{10,11},{11... | collective-permute-start | bytes 44 | tf_op jit(solution)/shard_map/neighbours/ppermute | solution.py:321
  62.0 13.9 %all-to-all-done.2.both_ref = f32[16,40,128]{2,1,0:T(8,128)S(1)} async-done(((f32[16,40,128]{2,1,0:T(8,128)}), f32[16,40,128]{2,1,0:T(8,128)S(1)}, u32[]{:S(2)}, u32[]{:S(2)}) %all-to-all-start.2) | async-done | bytes 327712 | tf_op jit(solution)/shard_map/sum_z/all_to_all | solution.py:298
  75.9 0.7 sum_z.1
  76.6 0.0 collective-permute-done.3.above_ref
  76.6 0.0 collective-permute-done.2.below_ref
  76.6 0.0 copy-start.4
  76.6 6.7 %all-to-all-start.3 = ((f32[16,24,128]{2,1,0:T(8,128)}), f32[16,24,128]{2,1,0:T(8,128)S(1)}, u32[]{:S(2)}, u32[]{:S(2)}) async-start(f32[16,24,128]{2,1,0:T(8,128)} %get-tuple-element.33), calls=%async_computation.3 | async-start | bytes 393216 | tf_op jit(solution)/shard_map/gather_z/all_to_all | solution.py:298
  83.4 0.0 copy-done.4
  83.4 8.5 %first_round.1 = (bf16[512,128]{1,0:T(8,128)(2,1)S(1)}, bf16[512,128]{1,0:T(8,128)(2,1)S(1)}, f32[128,128]{1,0:T(8,128)S(1)}) custom-call(s32[1]{0:T(128)} %bitcast.pair_ref, s32[8,13]{1,0:T(8,128)S(1)} %copy-done.4, s32[3]{0:T(128)S(1)} %bitcast.7, f32[256,128]{1,0:T(8,128)S(1)} %get-tuple-element.34.gram_ref, f32[8,128]{1,0:T(8,128)S(1)} %get-tuple-element.35.diagonal_ref), custom_call_target="tpu_custom_call" | custom-call | flops 8999999488 | tf_op jit(solution)/shard_map/first_round/pallas_call | solution.py:272
  91.9 1.5 %collective-permute-start.4 = (bf16[512,128]{1,0:T(8,128)(2,1)S(1)}, bf16[512,128]{1,0:T(8,128)(2,1)S(1)}, u32[]{:S(2)}, u32[]{:S(2)}) collective-permute-start(bf16[512,128]{1,0:T(8,128)(2,1)S(1)} %get-tuple-element.36.rest_3_), channel_id=1, source_target_pairs={{1,0},{0,2},{2,4},{4,6},{6,7},{7,5},{5,3},{3,1},{9,8},{8,10},{10,1... | collective-permute-start | bytes 393224 | tf_op jit(solution)/shard_map/neighbours/ppermute | solution.py:338
  93.4 0.0 collective-permute-start.5
  93.4 2.5 %collective-permute-done.4.from_left_ref.rest_1_ = bf16[512,128]{1,0:T(8,128)(2,1)S(1)} collective-permute-done((bf16[512,128]{1,0:T(8,128)(2,1)S(1)}, bf16[512,128]{1,0:T(8,128)(2,1)S(1)}, u32[]{:S(2)}, u32[]{:S(2)}) %collective-permute-start.4) | collective-permute-done | bytes 131104 | tf_op jit(solution)/shard_map/neighbours/ppermute | solution.py:338
  95.9 2.4 %collective-permute-done.5.from_right_ref.rest_4_ = bf16[512,128]{1,0:T(8,128)(2,1)S(1)} collective-permute-done((bf16[512,128]{1,0:T(8,128)(2,1)S(1)}, bf16[512,128]{1,0:T(8,128)(2,1)S(1)}, u32[]{:S(2)}, u32[]{:S(2)}) %collective-permute-start.5) | collective-permute-done | bytes 131104 | tf_op jit(solution)/shard_map/neighbours/ppermute | solution.py:339
  98.4 1.0 all-to-all-done.3
  99.4 0.2 gather_y.1
  99.6 9.8 %all_to_all.27.rest_0_ = f32[4,192,128]{2,1,0:T(8,128)S(1)} all-to-all(f32[4,192,128]{2,1,0:T(8,128)S(1)} %gather_y.1), channel_id=1, replica_groups={{0,8,16,24},{32,40,48,56},{64,72,80,88},{96,104,112,120},{128,136,144,1..., dimensions={0} | all-to-all | bytes 786432 | tf_op jit(solution)/shard_map/gather_y/all_to_all | solution.py:298
  109.4 20.3 %rounds.1 = (bf16[2048,256]{1,0:T(8,128)(2,1)}, f32[1,256]{1,0:T(1,128)}) custom-call(s32[1]{0:T(128)} %bitcast.pair_ref, s32[8,13]{1,0:T(8,128)S(1)} %copy-done.4, s32[3]{0:T(128)S(1)} %bitcast.8, s32[3]{0:T(128)S(1)} %collective-permute-done.2.below_ref, s32[3]{0:T(128)S(1)} %collective-permute-done.3.above_ref, f32[4,192,128]{2,1,0:T(8,128)S(1)} %all_to_all.27.rest_0_, ...), custom_call_target="tpu_custom_call" | custom-call | flops 20999999488 | tf_op jit(solution)/shard_map/rounds/pallas_call | solution.py:272
Async XLA Ops:
  0.6 34.6 %collective-permute-start.1 = (bf16[2048,256]{1,0:T(8,128)(2,1)}, bf16[2048,256]{1,0:T(8,128)(2,1)S(1)}, u32[]{:S(2)}, u32[]{:S(2)}) collective-permute-start(bf16[2048,256]{1,0:T(8,128)(2,1)} %rest_7_.1), channel_id=1, source_target_pairs={{0,1},{2,0},{4,2},{6,4},{7,6},{5,7},{3,5},{1,3},{8,9},{10,8},{12,1... | collective-permute-start | bytes 3145736 | tf_op jit(solution)/shard_map/neighbours/ppermute | solution.py:302
  0.7 34.6 %collective-permute-start = (bf16[2048,256]{1,0:T(8,128)(2,1)}, bf16[2048,256]{1,0:T(8,128)(2,1)S(1)}, u32[]{:S(2)}, u32[]{:S(2)}) collective-permute-start(bf16[2048,256]{1,0:T(8,128)(2,1)} %rest_7_.1), channel_id=1, source_target_pairs={{1,0},{0,2},{2,4},{4,6},{6,7},{7,5},{5,3},{3,1},{9,8},{8,10},{10,1... | collective-permute-start | bytes 3145736 | tf_op jit(solution)/shard_map/neighbours/ppermute | solution.py:301
  2.7 1.3 copy-start
  35.2 1.1 copy-start.1
  35.2 1.3 %copy-start.2 = (bf16[2048,256]{1,0:T(8,128)(2,1)}, bf16[2048,256]{1,0:T(8,128)(2,1)S(1)}, u32[]{:S(2)}) copy-start(bf16[2048,256]{1,0:T(8,128)(2,1)S(1)} %collective-permute-done.left_ref.rest_6_) | copy-start | bytes 3145732
  49.2 26.7 %all-to-all-start.2 = ((f32[16,40,128]{2,1,0:T(8,128)}), f32[16,40,128]{2,1,0:T(8,128)S(1)}, u32[]{:S(2)}, u32[]{:S(2)}) async-start(f32[16,40,128]{2,1,0:T(8,128)} %get-tuple-element.28), calls=%async_computation.2 | async-start | bytes 655360 | tf_op jit(solution)/shard_map/sum_z/all_to_all | solution.py:298
  57.0 0.7 copy-start.3
  57.7 19.0 %collective-permute-start.3 = (s32[3]{0:T(128)S(1)}, s32[3]{0:T(128)S(1)}, u32[]{:S(2)}, u32[]{:S(2)}) collective-permute-start(s32[3]{0:T(128)S(1)} %bitcast.5), channel_id=1, source_target_pairs={{1,0},{2,1},{3,2},{4,3},{5,4},{6,5},{7,6},{9,8},{10,9},{11,10},{12... | collective-permute-start | bytes 44 | tf_op jit(solution)/shard_map/neighbours/ppermute | solution.py:322
  58.9 17.7 %collective-permute-start.2 = (s32[3]{0:T(128)S(1)}, s32[3]{0:T(128)S(1)}, u32[]{:S(2)}, u32[]{:S(2)}) collective-permute-start(s32[3]{0:T(128)S(1)} %bitcast.6), channel_id=1, source_target_pairs={{0,1},{1,2},{2,3},{3,4},{4,5},{5,6},{6,7},{8,9},{9,10},{10,11},{11... | collective-permute-start | bytes 44 | tf_op jit(solution)/shard_map/neighbours/ppermute | solution.py:321
  76.6 6.7 %copy-start.4 = (s32[8,13]{1,0:T(8,128)S(1)}, s32[8,13]{1,0:T(8,128)}, u32[]{:S(2)}) copy-start(s32[8,13]{1,0:T(8,128)} %constant.6.clone.table_ref) | copy-start | bytes 1252
  76.6 22.7 %all-to-all-start.3 = ((f32[16,24,128]{2,1,0:T(8,128)}), f32[16,24,128]{2,1,0:T(8,128)S(1)}, u32[]{:S(2)}, u32[]{:S(2)}) async-start(f32[16,24,128]{2,1,0:T(8,128)} %get-tuple-element.33), calls=%async_computation.3 | async-start | bytes 393216 | tf_op jit(solution)/shard_map/gather_z/all_to_all | solution.py:298
  91.9 4.0 %collective-permute-start.4 = (bf16[512,128]{1,0:T(8,128)(2,1)S(1)}, bf16[512,128]{1,0:T(8,128)(2,1)S(1)}, u32[]{:S(2)}, u32[]{:S(2)}) collective-permute-start(bf16[512,128]{1,0:T(8,128)(2,1)S(1)} %get-tuple-element.36.rest_3_), channel_id=1, source_target_pairs={{1,0},{0,2},{2,4},{4,6},{6,7},{7,5},{5,3},{3,1},{9,8},{8,10},{10,1... | collective-permute-start | bytes 393224 | tf_op jit(solution)/shard_map/neighbours/ppermute | solution.py:338
  93.4 5.0 %collective-permute-start.5 = (bf16[512,128]{1,0:T(8,128)(2,1)S(1)}, bf16[512,128]{1,0:T(8,128)(2,1)S(1)}, u32[]{:S(2)}, u32[]{:S(2)}) collective-permute-start(bf16[512,128]{1,0:T(8,128)(2,1)S(1)} %get-tuple-element.37.rest_2_), channel_id=1, source_target_pairs={{0,1},{2,0},{4,2},{6,4},{7,6},{5,7},{3,5},{1,3},{8,9},{10,8},{12,1... | collective-permute-start | bytes 393224 | tf_op jit(solution)/shard_map/neighbours/ppermute | solution.py:339

commit v7 on v4

--- a/solution.py
+++ b/solution.py
@@ -162,9 +162,12 @@
 
 def cubed(iterate):
     high, low = split(iterate)
-    square = dot(high, high, NT) + dot(high, low, NT) + dot(low, high, NT)
+    order = iterate.shape[0]
+    tall = dot(jnp.concatenate([high, low], axis=0), high, NT)
+    square = tall[:order] + tall[order:] + dot(high, low, NT)
     sq_high, sq_low = split(square)
-    return dot(sq_high, high, NN) + dot(sq_low, high, NN) + dot(sq_high, low, NN)
+    tall = dot(jnp.concatenate([sq_high, sq_low], axis=0), high, NN)
+    return tall[:order] + tall[order:] + dot(sq_high, low, NN)
 
 
 def first_step(start):

time: 130 us -> 130 us (level)
  transfers between devices with their start and end apart: 8 -> 8, of which waited for: 4 -> 4; matrix products, arithmetic and copies ran while one was open for 0% -> 0% of each run, Pallas kernels for 8% -> 7%
where the time goes in v7:
time: 130 us; the launch traced here: 129 us
  blocking collectives  52.5 us (40%)
  Pallas kernels  31.3 us (24%)
  starting transfers between devices  22.3 us (17%)
  waiting for transfers between devices  20 us (15%)
  local copies, waits for them, and re-layouts  2.19 us (2%)
    all_to_all x3, blocking collectives, swapped(): lax.all_to_all(value.reshape(count, -1, HALF), 'rows', 0, 0, axis_index_g...  52.5 us
    pallas_call x7, Pallas kernels, call(): pl.pallas_call(kernel, out_shape=outs, in_specs=[pl.BlockSpec(memory_spac...  31.3 us
    all_to_all x2, waiting for transfers between devices, swapped(): lax.all_to_all(value.reshape(count, -1, HALF), 'rows', 0, 0, axis_index_g...  15 us
    all_to_all x2, starting transfers between devices, swapped(): lax.all_to_all(value.reshape(count, -1, HALF), 'rows', 0, 0, axis_index_g...  14.5 us
    ppermute x1, starting transfers between devices, per_device(): below = lax.ppermute(orient, 'cols', [(c - 1, c) for c in range(1, pairs)])  3.03 us
  transfers between devices with their start and end apart: 8, of which 4 were waited for; matrix products, arithmetic and copies ran while one was open for 0% of the time, Pallas kernels for 7%

profile of v7, /device:TPU:32, one launch (start us, length us, event | category | flops | bytes accessed | tf_op | source)
XLA Modules:
  0.0 129.2 jit_solution(13248307533345855845)
XLA Ops:
  0.6 0.0 collective-permute-start.1
  0.7 2.0 %collective-permute-start = (bf16[2048,256]{1,0:T(8,128)(2,1)}, bf16[2048,256]{1,0:T(8,128)(2,1)S(1)}, u32[]{:S(2)}, u32[]{:S(2)}) collective-permute-start(bf16[2048,256]{1,0:T(8,128)(2,1)} %rest_7_.1), channel_id=1, source_target_pairs={{1,0},{0,2},{2,4},{4,6},{6,7},{7,5},{5,3},{3,1},{9,8},{8,10},{10,1... | collective-permute-start | bytes 3145736 | tf_op jit(solution)/shard_map/neighbours/ppermute | solution.py:307
  2.7 0.0 copy-start
  2.7 1.3 copy-done
  3.9 0.5 own_gram.1
  4.4 30.8 %all_to_all.25.gram_ref = f32[16,24,128]{2,1,0:T(8,128)S(1)} all-to-all(f32[16,24,128]{2,1,0:T(8,128)S(1)} %own_gram.1), channel_id=1, replica_groups={{0,32,64,96,128,160,192,224,256,288,320,352,384,416,448,480},{8,40,72,1..., dimensions={0} | all-to-all | bytes 393216 | tf_op jit(solution)/shard_map/own_gram/all_to_all | solution.py:304
  35.2 0.0 collective-permute-done.1.right_ref.rest_8_
  35.2 0.0 copy-start.1
  35.2 0.0 collective-permute-done.left_ref.rest_6_
  35.2 0.0 copy-start.2
  35.2 1.0 sum_y.2
  36.3 0.0 copy-done.1
  36.3 0.3 copy-done.2
  36.6 11.9 %all_to_all.26.both_ref = bf16[4,432,128]{2,1,0:T(8,128)(2,1)S(1)} all-to-all(bf16[4,432,128]{2,1,0:T(8,128)(2,1)S(1)} %sum_y.2), channel_id=1, replica_groups={{0,8,16,24},{32,40,48,56},{64,72,80,88},{96,104,112,120},{128,136,144,1..., dimensions={0} | all-to-all | bytes 884736 | tf_op jit(solution)/shard_map/sum_y/all_to_all | solution.py:304
  48.5 0.8 sum_y.3
  49.2 7.8 %all-to-all-start.2 = ((f32[16,40,128]{2,1,0:T(8,128)}), f32[16,40,128]{2,1,0:T(8,128)S(1)}, u32[]{:S(2)}, u32[]{:S(2)}) async-start(f32[16,40,128]{2,1,0:T(8,128)} %get-tuple-element.28), calls=%async_computation.2 | async-start | bytes 655360 | tf_op jit(solution)/shard_map/sum_z/all_to_all | solution.py:304
  57.0 0.0 copy-start.3
  57.0 0.6 copy-done.3
  57.7 1.3 collective-permute-start.3
  58.9 3.0 %collective-permute-start.2 = (s32[3]{0:T(128)S(1)}, s32[3]{0:T(128)S(1)}, u32[]{:S(2)}, u32[]{:S(2)}) collective-permute-start(s32[3]{0:T(128)S(1)} %bitcast.6), channel_id=1, source_target_pairs={{0,1},{1,2},{2,3},{3,4},{4,5},{5,6},{6,7},{8,9},{9,10},{10,11},{11... | collective-permute-start | bytes 44 | tf_op jit(solution)/shard_map/neighbours/ppermute | solution.py:327
  62.0 13.9 %all-to-all-done.2.both_ref = f32[16,40,128]{2,1,0:T(8,128)S(1)} async-done(((f32[16,40,128]{2,1,0:T(8,128)}), f32[16,40,128]{2,1,0:T(8,128)S(1)}, u32[]{:S(2)}, u32[]{:S(2)}) %all-to-all-start.2) | async-done | bytes 327712 | tf_op jit(solution)/shard_map/sum_z/all_to_all | solution.py:304
  75.9 0.7 sum_z.1
  76.6 0.0 collective-permute-done.3.above_ref
  76.6 0.0 collective-permute-done.2.below_ref
  76.6 0.0 copy-start.4
  76.6 6.7 %all-to-all-start.3 = ((f32[16,24,128]{2,1,0:T(8,128)}), f32[16,24,128]{2,1,0:T(8,128)S(1)}, u32[]{:S(2)}, u32[]{:S(2)}) async-start(f32[16,24,128]{2,1,0:T(8,128)} %get-tuple-element.33), calls=%async_computation.3 | async-start | bytes 393216 | tf_op jit(solution)/shard_map/gather_z/all_to_all | solution.py:304
  83.4 0.0 copy-done.4
  83.4 8.4 %first_round.1 = (bf16[512,128]{1,0:T(8,128)(2,1)S(1)}, bf16[512,128]{1,0:T(8,128)(2,1)S(1)}, f32[128,128]{1,0:T(8,128)S(1)}) custom-call(s32[1]{0:T(128)} %bitcast.pair_ref, s32[8,13]{1,0:T(8,128)S(1)} %copy-done.4, s32[3]{0:T(128)S(1)} %bitcast.7, f32[256,128]{1,0:T(8,128)S(1)} %get-tuple-element.34.gram_ref, f32[8,128]{1,0:T(8,128)S(1)} %get-tuple-element.35.diagonal_ref), custom_call_target="tpu_custom_call" | custom-call | flops 8999999488 | tf_op jit(solution)/shard_map/first_round/pallas_call | solution.py:278
  91.8 1.5 %collective-permute-start.4 = (bf16[512,128]{1,0:T(8,128)(2,1)S(1)}, bf16[512,128]{1,0:T(8,128)(2,1)S(1)}, u32[]{:S(2)}, u32[]{:S(2)}) collective-permute-start(bf16[512,128]{1,0:T(8,128)(2,1)S(1)} %get-tuple-element.36.rest_3_), channel_id=1, source_target_pairs={{1,0},{0,2},{2,4},{4,6},{6,7},{7,5},{5,3},{3,1},{9,8},{8,10},{10,1... | collective-permute-start | bytes 393224 | tf_op jit(solution)/shard_map/neighbours/ppermute | solution.py:344
  93.3 0.0 collective-permute-start.5
  93.3 2.5 %collective-permute-done.4.from_left_ref.rest_1_ = bf16[512,128]{1,0:T(8,128)(2,1)S(1)} collective-permute-done((bf16[512,128]{1,0:T(8,128)(2,1)S(1)}, bf16[512,128]{1,0:T(8,128)(2,1)S(1)}, u32[]{:S(2)}, u32[]{:S(2)}) %collective-permute-start.4) | collective-permute-done | bytes 131104 | tf_op jit(solution)/shard_map/neighbours/ppermute | solution.py:344
  95.8 2.4 %collective-permute-done.5.from_right_ref.rest_4_ = bf16[512,128]{1,0:T(8,128)(2,1)S(1)} collective-permute-done((bf16[512,128]{1,0:T(8,128)(2,1)S(1)}, bf16[512,128]{1,0:T(8,128)(2,1)S(1)}, u32[]{:S(2)}, u32[]{:S(2)}) %collective-permute-start.5) | collective-permute-done | bytes 131104 | tf_op jit(solution)/shard_map/neighbours/ppermute | solution.py:345
  98.3 1.1 all-to-all-done.3
  99.4 0.2 gather_y.1
  99.6 9.8 %all_to_all.27.rest_0_ = f32[4,192,128]{2,1,0:T(8,128)S(1)} all-to-all(f32[4,192,128]{2,1,0:T(8,128)S(1)} %gather_y.1), channel_id=1, replica_groups={{0,8,16,24},{32,40,48,56},{64,72,80,88},{96,104,112,120},{128,136,144,1..., dimensions={0} | all-to-all | bytes 786432 | tf_op jit(solution)/shard_map/gather_y/all_to_all | solution.py:304
  109.4 19.7 %rounds.1 = (bf16[2048,256]{1,0:T(8,128)(2,1)}, f32[1,256]{1,0:T(1,128)}) custom-call(s32[1]{0:T(128)} %bitcast.pair_ref, s32[8,13]{1,0:T(8,128)S(1)} %copy-done.4, s32[3]{0:T(128)S(1)} %bitcast.8, s32[3]{0:T(128)S(1)} %collective-permute-done.2.below_ref, s32[3]{0:T(128)S(1)} %collective-permute-done.3.above_ref, f32[4,192,128]{2,1,0:T(8,128)S(1)} %all_to_all.27.rest_0_, ...), custom_call_target="tpu_custom_call" | custom-call | flops 20999999488 | tf_op jit(solution)/shard_map/rounds/pallas_call | solution.py:278
Async XLA Ops:
  0.6 34.6 %collective-permute-start.1 = (bf16[2048,256]{1,0:T(8,128)(2,1)}, bf16[2048,256]{1,0:T(8,128)(2,1)S(1)}, u32[]{:S(2)}, u32[]{:S(2)}) collective-permute-start(bf16[2048,256]{1,0:T(8,128)(2,1)} %rest_7_.1), channel_id=1, source_target_pairs={{0,1},{2,0},{4,2},{6,4},{7,6},{5,7},{3,5},{1,3},{8,9},{10,8},{12,1... | collective-permute-start | bytes 3145736 | tf_op jit(solution)/shard_map/neighbours/ppermute | solution.py:308
  0.7 34.6 %collective-permute-start = (bf16[2048,256]{1,0:T(8,128)(2,1)}, bf16[2048,256]{1,0:T(8,128)(2,1)S(1)}, u32[]{:S(2)}, u32[]{:S(2)}) collective-permute-start(bf16[2048,256]{1,0:T(8,128)(2,1)} %rest_7_.1), channel_id=1, source_target_pairs={{1,0},{0,2},{2,4},{4,6},{6,7},{7,5},{5,3},{3,1},{9,8},{8,10},{10,1... | collective-permute-start | bytes 3145736 | tf_op jit(solution)/shard_map/neighbours/ppermute | solution.py:307
  2.7 1.3 copy-start
  35.2 1.1 copy-start.1
  35.2 1.3 %copy-start.2 = (bf16[2048,256]{1,0:T(8,128)(2,1)}, bf16[2048,256]{1,0:T(8,128)(2,1)S(1)}, u32[]{:S(2)}) copy-start(bf16[2048,256]{1,0:T(8,128)(2,1)S(1)} %collective-permute-done.left_ref.rest_6_) | copy-start | bytes 3145732
  49.2 26.7 %all-to-all-start.2 = ((f32[16,40,128]{2,1,0:T(8,128)}), f32[16,40,128]{2,1,0:T(8,128)S(1)}, u32[]{:S(2)}, u32[]{:S(2)}) async-start(f32[16,40,128]{2,1,0:T(8,128)} %get-tuple-element.28), calls=%async_computation.2 | async-start | bytes 655360 | tf_op jit(solution)/shard_map/sum_z/all_to_all | solution.py:304
  57.0 0.7 copy-start.3
  57.7 19.0 %collective-permute-start.3 = (s32[3]{0:T(128)S(1)}, s32[3]{0:T(128)S(1)}, u32[]{:S(2)}, u32[]{:S(2)}) collective-permute-start(s32[3]{0:T(128)S(1)} %bitcast.5), channel_id=1, source_target_pairs={{1,0},{2,1},{3,2},{4,3},{5,4},{6,5},{7,6},{9,8},{10,9},{11,10},{12... | collective-permute-start | bytes 44 | tf_op jit(solution)/shard_map/neighbours/ppermute | solution.py:328
  58.9 17.7 %collective-permute-start.2 = (s32[3]{0:T(128)S(1)}, s32[3]{0:T(128)S(1)}, u32[]{:S(2)}, u32[]{:S(2)}) collective-permute-start(s32[3]{0:T(128)S(1)} %bitcast.6), channel_id=1, source_target_pairs={{0,1},{1,2},{2,3},{3,4},{4,5},{5,6},{6,7},{8,9},{9,10},{10,11},{11... | collective-permute-start | bytes 44 | tf_op jit(solution)/shard_map/neighbours/ppermute | solution.py:327
  76.6 6.7 %copy-start.4 = (s32[8,13]{1,0:T(8,128)S(1)}, s32[8,13]{1,0:T(8,128)}, u32[]{:S(2)}) copy-start(s32[8,13]{1,0:T(8,128)} %constant.6.clone.table_ref) | copy-start | bytes 1252
  76.6 22.7 %all-to-all-start.3 = ((f32[16,24,128]{2,1,0:T(8,128)}), f32[16,24,128]{2,1,0:T(8,128)S(1)}, u32[]{:S(2)}, u32[]{:S(2)}) async-start(f32[16,24,128]{2,1,0:T(8,128)} %get-tuple-element.33), calls=%async_computation.3 | async-start | bytes 393216 | tf_op jit(solution)/shard_map/gather_z/all_to_all | solution.py:304
  91.8 4.0 %collective-permute-start.4 = (bf16[512,128]{1,0:T(8,128)(2,1)S(1)}, bf16[512,128]{1,0:T(8,128)(2,1)S(1)}, u32[]{:S(2)}, u32[]{:S(2)}) collective-permute-start(bf16[512,128]{1,0:T(8,128)(2,1)S(1)} %get-tuple-element.36.rest_3_), channel_id=1, source_target_pairs={{1,0},{0,2},{2,4},{4,6},{6,7},{7,5},{5,3},{3,1},{9,8},{8,10},{10,1... | collective-permute-start | bytes 393224 | tf_op jit(solution)/shard_map/neighbours/ppermute | solution.py:344
  93.3 5.0 %collective-permute-start.5 = (bf16[512,128]{1,0:T(8,128)(2,1)S(1)}, bf16[512,128]{1,0:T(8,128)(2,1)S(1)}, u32[]{:S(2)}, u32[]{:S(2)}) collective-permute-start(bf16[512,128]{1,0:T(8,128)(2,1)S(1)} %get-tuple-element.37.rest_2_), channel_id=1, source_target_pairs={{0,1},{2,0},{4,2},{6,4},{7,6},{5,7},{3,5},{1,3},{8,9},{10,8},{12,1... | collective-permute-start | bytes 393224 | tf_op jit(solution)/shard_map/neighbours/ppermute | solution.py:345
